TPU v7x, 32 devices: a whole 2x2x4 slice. The times are simulated.
32 devices in a mesh: row: 4 (over y, x), col: 8 (over z, core).
Axes of the slice: x: 2, y: 2, z: 4, core: 2. Of those that a mesh axis runs over, the one named last changes fastest.
Arguments:
- tokens: bfloat16 [256, 16384], P('col', 'row'), may hold values from -6 to 6
- gate_weight: bfloat16 [16384, 28672], P('row', 'col'), may hold values from -0.078125 to 0.078125
- up_weight: bfloat16 [16384, 28672], P('row', 'col'), may hold values from -0.078125 to 0.078125
- down_weight: bfloat16 [28672, 16384], P('col', 'row'), may hold values from -0.0625 to 0.0625
- gate_mask: int32 [128, 224], P('row', 'col'), may hold values from 0 to 1, as said below
- up_mask: int32 [128, 224], P('row', 'col'), may hold values from 0 to 1, as said below
- down_mask: int32 [224, 128], P('col', 'row'), may hold values from 0 to 1, as said below
Outputs:
- mixed_output: bfloat16 [256, 16384], P('col', 'row')
Inputs may be any that keep to these rules, and one draw needn't show every extreme that they name: `gate_mask`: 1 keeps a 128 x 128 block of the weight, 0 drops it. `up_mask`: 1 keeps a 128 x 128 block of the weight, 0 drops it. `down_mask`: 1 keeps a 128 x 128 block of the weight, 0 drops it.
All inputs are finite; a program needn't handle non-finite values.
Results may differ from a plain program's by a relative error of at most 0.0049.
Values may be sent and summed in bfloat16 or wider, within the bound.
No kernel may reach another device: no remote copies, remote signals or barrier semaphores. Data moves between devices by JAX's collectives and lax.ppermute only.
A program may use at most 256 MiB of HBM per device.

v0:
```python
import jax
import jax.numpy as jnp
from jax import lax
from jax.sharding import PartitionSpec as P


def apply_blocks(weight, mask):
    block_rows, block_cols = mask.shape
    shaped = weight.reshape(
        block_rows, weight.shape[0] // block_rows, block_cols, weight.shape[1] // block_cols
    )
    kept = shaped * mask.astype(weight.dtype)[:, None, :, None]
    return kept.reshape(weight.shape)


def on_device(tokens, gate_weight, up_weight, down_weight, gate_mask, up_mask, down_mask):
    gate_kept = apply_blocks(gate_weight, gate_mask)
    up_kept = apply_blocks(up_weight, up_mask)
    down_kept = apply_blocks(down_weight, down_mask)
    panel_rows = lax.all_gather(tokens, "col", axis=0, tiled=True)
    gate_part = jnp.dot(panel_rows, gate_kept, preferred_element_type=jnp.float32)
    up_part = jnp.dot(panel_rows, up_kept, preferred_element_type=jnp.float32)
    partial_sums = jnp.stack([gate_part, up_part])
    summed = lax.psum(partial_sums, "row")
    hidden = (jax.nn.silu(summed[0]) * summed[1]).astype(jnp.bfloat16)
    output_rows = lax.psum_scatter(
        jnp.dot(hidden, down_kept, preferred_element_type=jnp.float32),
        "col",
        scatter_dimension=0,
        tiled=True,
    )
    return output_rows.astype(jnp.bfloat16)


def solution(mesh):
    return jax.shard_map(
        on_device,
        mesh=mesh,
        in_specs=(
            P("col", "row"),
            P("row", "col"),
            P("row", "col"),
            P("col", "row"),
            P("row", "col"),
            P("row", "col"),
            P("col", "row"),
        ),
        out_specs=P("col", "row"),
        check_vma=False,
    )
```

profile of v0, /device:TPU:0, one launch (start us, length us, event | category | flops | bytes accessed | tf_op | source)
XLA Modules:
  0.0 413.5 jit_solution(13046461507577735882)
XLA Ops:
  6.5 0.0 all-gather.2.cloned.1.call-start
  6.5 0.7 all-gather.2.cloned.1.call-update
  7.3 0.0 all-reduce.2.cloned.1.call-start
  7.3 0.7 convert_element_type.15
  8.0 0.1 copy.8
  8.1 38.8 %copy.9 = bf16[4096,3584]{0,1:T(8,128)(2,1)} copy(bf16[4096,3584]{1,0:T(8,128)(2,1)} %param.8) | data formatting | bytes 58720256 | tf_op args[1]
  47.0 0.0 copy-done
  47.0 0.1 copy.10
  47.1 37.2 %copy.11 = bf16[4096,3584]{0,1:T(8,128)(2,1)} copy(bf16[4096,3584]{1,0:T(8,128)(2,1)} %param.9) | data formatting | bytes 58720256 | tf_op args[2]
  84.3 10.0 %mul.40 = bf16[32,128,28,128]{1,0,3,2:T(8,128)(2,1)} broadcast(bf16[32,28]{0,1:T(8,128)(2,1)S(1)} %copy.8), dimensions={0,2} | broadcast | bytes 29361920 | tf_op jit(solution)/shard_map/mul | solution.py:12
  94.2 0.0 copy-done.2
  94.2 22.5 %fusion.6 = f32[1,256,3584]{1,2,0:T(8,128)} fusion(bf16[256,4096]{1,0:T(8,128)(2,1)S(1)} %copy-done.2, bf16[4096,3584]{0,1:T(8,128)(2,1)} %copy.9, bf16[448,8,32,128]{3,2,1,0:T(8,128)(2,1)} %bitcast.46), kind=kOutput, calls=%fused_computation.10 | convolution fusion | flops 7530872832 | bytes 64487424 | tf_op jit(solution)/shard_map/dot_general | solution.py:21
  116.8 9.8 %mul.43 = bf16[32,128,28,128]{1,0,3,2:T(8,128)(2,1)} broadcast(bf16[32,28]{0,1:T(8,128)(2,1)S(1)} %copy.10), dimensions={0,2} | broadcast | bytes 29361920 | tf_op jit(solution)/shard_map/mul | solution.py:12
  126.6 22.5 %fusion.7 = f32[1,256,3584]{1,2,0:T(8,128)} fusion(bf16[256,4096]{1,0:T(8,128)(2,1)S(1)} %copy-done.2, bf16[4096,3584]{0,1:T(8,128)(2,1)} %copy.11, bf16[448,8,32,128]{3,2,1,0:T(8,128)(2,1)} %bitcast.45), kind=kOutput, calls=%fused_computation.11 | convolution fusion | flops 7530872832 | bytes 64487424 | tf_op jit(solution)/shard_map/dot_general | solution.py:22
  149.1 6.6 %pad_maximum_fusion = f32[2,256,3584]{1,2,0:T(8,128)} fusion(f32[1,256,3584]{1,2,0:T(8,128)} %fusion.7, f32[1,256,3584]{1,2,0:T(8,128)} %fusion.6), kind=kLoop, calls=%fused_computation.9 | loop fusion | flops 1835008 | bytes 14680064 | tf_op jit(solution)/shard_map/stack | solution.py:23
  155.7 0.0 all-reduce.2.cloned.1.call-update
  155.7 0.2 reduce-scatter.2.cloned.1.call-start
  155.9 0.5 copy-done.1
  156.4 158.9 %all-reduce.2.cloned.1.call-done = f32[2,256,3584]{1,2,0:T(8,128)} async-done(((f32[2,256,3584]{1,2,0:T(8,128)}), f32[2,256,3584]{1,2,0:T(8,128)}) %all-reduce.2.cloned.1.call-update) | async-done | bytes 7340048 | tf_op jit(solution)/shard_map/psum | solution.py:24
  315.3 9.9 %mul.48 = bf16[28,128,32,128]{3,2,1,0:T(8,128)(2,1)} broadcast(bf16[28,32]{1,0:T(8,128)(2,1)S(1)} %convert_element_type.18), dimensions={0,2} | broadcast | bytes 29361920 | tf_op jit(solution)/shard_map/mul | solution.py:12
  325.2 29.8 %fusion = f32[256,4096]{1,0:T(8,128)} fusion(bf16[3584,4096]{1,0:T(8,128)(2,1)} %param.10, bf16[448,8,32,128]{3,2,1,0:T(8,128)(2,1)} %bitcast.47, f32[2,256,3584]{1,2,0:T(8,128)} %all-reduce.2.cloned.1.call-done), kind=kOutput, calls=%fused_computation.1 | convolution fusion | flops 7536377856 | bytes 70254592 | tf_op jit(solution)/shard_map/dot_general | solution.py:27
  355.0 0.0 reduce-scatter.2.cloned.1.call-update
  355.0 50.2 %reduce-scatter.2.cloned.1.call-done = f32[32,4096]{1,0:T(8,128)} async-done(((f32[256,4096]{1,0:T(8,128)}), f32[32,4096]{1,0:T(8,128)}) %reduce-scatter.2.cloned.1.call-update) | async-done | bytes 524304 | tf_op jit(solution)/shard_map/reduce_scatter | solution.py:26
  405.2 1.8 convert_element_type.19
  (6 shorter events, 0.0 us)
Async XLA Ops:
  6.5 77.7 %all-gather.2.cloned.1.call-start = ((), (), s32[]{:S(2)}) async-start(), calls=%async_computation.1 | async-start | bytes 2359296 | tf_op jit(solution)/shard_map/all_gather | solution.py:20
  7.3 308.0 %all-reduce.2.cloned.1.call-start = ((), (), s32[]{:S(2)}) async-start(), calls=%async_computation.2 | async-start | bytes 14680064 | tf_op jit(solution)/shard_map/psum | solution.py:24
  8.1 38.9 %copy-start = (s32[32,28]{1,0:T(8,128)S(1)}, s32[32,28]{1,0:T(8,128)}, u32[]{:S(2)}) copy-start(s32[32,28]{1,0:T(8,128)} %param.12) | copy-start | bytes 10756
  84.2 10.0 %copy-start.2 = (bf16[256,4096]{1,0:T(8,128)(2,1)S(1)}, bf16[256,4096]{1,0:T(8,128)(2,1)}, u32[]{:S(2)}) copy-start(bf16[256,4096]{1,0:T(8,128)(2,1)} %all-gather.2.cloned.1.call-done) | copy-start | bytes 6291460
  155.6 0.7 copy-start.1
  155.7 249.5 %reduce-scatter.2.cloned.1.call-start = ((), (), s32[]{:S(2)}) async-start(), calls=%async_computation.3 | async-start | bytes 4718592 | tf_op jit(solution)/shard_map/reduce_scatter | solution.py:26
Sparse Core Ops, SparseCore 0:
  9.0 31.7 all-gather.1
  155.8 159.4 all-reduce.1
  355.1 49.9 reduce-scatter.1
where the time goes:
time: 416 us; the launch traced here: 413 us
  waiting for transfers between devices  210 us (50%)
  local copies, waits for them, and re-layouts  106 us (25%)
  matrix products  74.8 us (18%)
  between operations  13.1 us (3%)
  other arithmetic  9.08 us (2%)
    psum x1, waiting for transfers between devices, on_device(): summed = lax.psum(partial_sums, 'row')  159 us
    unnamed x8, local copies, waits for them, and re-layouts  76.5 us
    reduce_scatter x1, waiting for transfers between devices, on_device(): lax.psum_scatter(jnp.dot(hidden, down_kept, preferred_element_type=jnp.fl...  50.2 us
    dot_general x1, matrix products, on_device(): jnp.dot(hidden, down_kept, preferred_element_type=jnp.float32)  29.8 us
    mul x3, local copies, waits for them, and re-layouts, apply_blocks(): kept = shaped * mask.astype(weight.dtype)[:, None, :, None]  29.7 us
    dot_general x1, matrix products, on_device(): jnp.dot(panel_rows, gate_kept, preferred_element_type=jnp.float32)  22.5 us
    dot_general x1, matrix products, on_device(): up_part = jnp.dot(panel_rows, up_kept, preferred_element_type=jnp.float32)  22.5 us
  transfers between devices with their start and end apart: 3, of which 2 were waited for; matrix products, arithmetic and copies ran while one was open for 19% of the time, Pallas kernels for 0%

commit v1 on v0

v1 whole, which is shorter than its diff:
```python
import functools

import jax
import jax.numpy as jnp
from jax import lax
from jax.experimental import pallas as pl
from jax.experimental.pallas import tpu as pltpu
from jax.sharding import PartitionSpec as P

BF16 = jnp.bfloat16
F32 = jnp.float32
MIB = 1 << 20


def apply_blocks(weight, mask):
    block_rows, block_cols = mask.shape
    shaped = weight.reshape(
        block_rows, weight.shape[0] // block_rows, block_cols, weight.shape[1] // block_cols
    )
    kept = shaped * mask.astype(weight.dtype)[:, None, :, None]
    return kept.reshape(weight.shape)


def plain(tokens, gate_weight, up_weight, down_weight, gate_mask, up_mask, down_mask):
    rows = lax.all_gather(tokens, "col", axis=0, tiled=True)
    gate = jnp.dot(rows, apply_blocks(gate_weight, gate_mask), preferred_element_type=F32)
    up = jnp.dot(rows, apply_blocks(up_weight, up_mask), preferred_element_type=F32)
    gate, up = lax.psum(jnp.stack([gate, up]), "row")
    hidden = (jax.nn.silu(gate) * up).astype(BF16)
    part = jnp.dot(hidden, apply_blocks(down_weight, down_mask), preferred_element_type=F32)
    return lax.psum_scatter(part, "col", scatter_dimension=0, tiled=True).astype(BF16)


VMEM_SPEC = pl.BlockSpec(memory_space=pltpu.VMEM)
HBM_SPEC = pl.BlockSpec(memory_space=pltpu.HBM)
ANY_SPEC = pl.BlockSpec(memory_space=pl.ANY)


def in_hbm(value):
    return pltpu.with_memory_space_constraint(value, pltpu.HBM)


def in_vmem(value):
    return pltpu.with_memory_space_constraint(value, pltpu.VMEM)


def factor(mask, i, j):
    return mask[i, j].astype(F32).astype(BF16)


def loop(count, step, unroll=1):
    def body(i, carry):
        step(i)
        return carry

    lax.fori_loop(0, count, body, 0, unroll=unroll)


def cost(flops, count):
    return pl.CostEstimate(flops=flops, bytes_accessed=count, transcendentals=0)


def nothing(*refs):
    del refs


def tie(value, *deps):
    return pl.pallas_call(
        nothing,
        in_specs=[ANY_SPEC] * (1 + len(deps)),
        out_specs=ANY_SPEC,
        out_shape=jax.ShapeDtypeStruct(value.shape, value.dtype),
        input_output_aliases={0: 0},
        compiler_params=pltpu.CompilerParams(vmem_limit_bytes=MIB),
        name="tie",
    )(value, *deps)


def quarter_of(name):
    row, col = lax.axis_index("row"), lax.axis_index("col")
    step1 = 1 + lax.rem(col, 2)
    flip = {"own": 0, "second": 3 - step1, "first": step1, "last": 3}[name]
    return row ^ flip


class Pairs:
    def __init__(self, quarter, masks, weights, buf, held_masks, sem, mask_sem):
        self.quarter, self.masks, self.weights = quarter, masks, weights
        self.buf, self.held_masks, self.sem, self.mask_sem = buf, held_masks, sem, mask_sem
        self.tiles, self.depth, self.wide = buf.shape
        self.blk = self.wide // 2

    def mask_copies(self):
        return [
            pltpu.make_async_copy(m, h, self.mask_sem.at[t])
            for t, (m, h) in enumerate(zip(self.masks, self.held_masks))
        ]

    def copies(self, tile):
        column = pl.multiple_of((self.quarter * self.tiles + tile) * self.blk, self.blk)
        return [
            pltpu.make_async_copy(
                w.at[:, pl.ds(column, self.blk)],
                self.buf.at[tile, :, pl.ds(t * self.blk, self.blk)],
                self.sem.at[tile, t],
            )
            for t, w in enumerate(self.weights)
        ]

    def start(self):
        for copy in self.mask_copies():
            copy.start()

        def step(tile):
            for copy in self.copies(tile):
                copy.start()

        loop(self.tiles, step)
        for copy in self.mask_copies():
            copy.wait()

    def wait(self, tile):
        for copy in self.copies(tile):
            copy.wait()

    def masked(self, tile):
        blk = self.blk
        column = self.quarter * self.tiles + tile
        return [
            [
                self.buf[tile, a * blk : (a + 1) * blk, t * blk : (t + 1) * blk] * factor(m, a, column)
                for t, m in enumerate(self.held_masks)
            ]
            for a in range(self.depth // blk)
        ]


def pairs_scratch(mask, tiles):
    return [
        pltpu.SMEM(mask.shape, mask.dtype),
        pltpu.SMEM(mask.shape, mask.dtype),
        pltpu.SemaphoreType.DMA((tiles, 2)),
        pltpu.SemaphoreType.DMA((2,)),
    ]


def put_pair(out, tile, value):
    blk = value.shape[1] // 2
    half = out.shape[1] // 2
    for t in range(2):
        column = pl.multiple_of(t * half + tile * blk, blk)
        out[:, pl.ds(column, blk)] = value[:, t * blk : (t + 1) * blk].astype(out.dtype)


def get_pair(got, tile, blk):
    half = got[0].shape[1] // 2
    columns = [pl.ds(pl.multiple_of(t * half + tile * blk, blk), blk) for t in range(2)]
    return jnp.concatenate(
        [jnp.concatenate([part[:, at].astype(F32) for at in columns], axis=1) for part in got], axis=0
    )


def load_pairs_kernel(name, *refs):
    buf, *held_masks, sem, mask_sem = refs[-5:]
    pairs = Pairs(quarter_of(name), refs[:2], refs[2:4], buf, held_masks, sem, mask_sem)
    blk = pairs.blk
    pairs.start()

    def keep(tile):
        pairs.wait(tile)
        for a, blocks in enumerate(pairs.masked(tile)):
            for t, value in enumerate(blocks):
                buf[tile, a * blk : (a + 1) * blk, t * blk : (t + 1) * blk] = value

    loop(pairs.tiles, keep)


def load_pairs(name, masks, weights, deps=()):
    depth, width = weights[0].shape
    blk = width // masks[0].shape[1]
    tiles = masks[0].shape[1] // 4
    return pl.pallas_call(
        functools.partial(load_pairs_kernel, name),
        in_specs=[HBM_SPEC] * 4 + [ANY_SPEC] * len(deps),
        out_specs=VMEM_SPEC,
        out_shape=pltpu.VMEM((tiles, depth, 2 * blk), BF16),
        scratch_shapes=pairs_scratch(masks[0], tiles),
        compiler_params=pltpu.CompilerParams(vmem_limit_bytes=4 * MIB),
        cost_estimate=cost(0, 2 * 2 * depth * width // 4),
        name="load_" + name,
    )(*[in_hbm(v) for v in (*masks, *weights)], *deps)


def held_pairs_kernel(count, added, *refs):
    x, buf, got, out = refs[:count], refs[count], refs[count + 1 : count + 1 + added], refs[-1]

    def step(tile):
        rows = jnp.concatenate([part[...] for part in x], axis=0)
        value = jnp.dot(rows, buf[tile], preferred_element_type=F32)
        if added:
            value = value + get_pair(got, tile, buf.shape[2] // 2)
        put_pair(out, tile, value)

    loop(buf.shape[0], step, unroll=buf.shape[0])


def held_pairs(x, buf, added=(), deps=()):
    tiles, depth, wide = buf.shape
    rows = sum(part.shape[0] for part in x)
    return pl.pallas_call(
        functools.partial(held_pairs_kernel, len(x), len(added)),
        in_specs=[VMEM_SPEC] * (len(x) + 1 + len(added)) + [ANY_SPEC] * len(deps),
        out_specs=VMEM_SPEC,
        out_shape=jax.ShapeDtypeStruct((rows, tiles * wide), BF16),
        compiler_params=pltpu.CompilerParams(vmem_limit_bytes=4 * MIB),
        cost_estimate=cost(2 * rows * depth * tiles * wide, 2 * tiles * depth * wide // 2),
        name="held_pairs",
    )(*[in_vmem(part) for part in x], in_vmem(buf), *[in_vmem(part) for part in added], *deps)


def stream_pairs_kernel(name, count, rows, *refs):
    x, outs = refs[4 : 4 + count], refs[-5 - len(rows) : -5]
    buf, *held_masks, sem, mask_sem = refs[-5:]
    pairs = Pairs(quarter_of(name), refs[:2], refs[2:4], buf, held_masks, sem, mask_sem)
    pairs.start()

    def step(tile):
        pairs.wait(tile)
        w = jnp.concatenate([jnp.concatenate(row, axis=1) for row in pairs.masked(tile)], axis=0)
        value = jnp.dot(jnp.concatenate([part[...] for part in x], axis=0), w, preferred_element_type=F32)
        first = 0
        for size, out in zip(rows, outs):
            put_pair(out, tile, value[first : first + size])
            first += size

    loop(pairs.tiles, step)


def stream_pairs(name, masks, weights, groups, deps=()):
    depth, width = weights[0].shape
    blk = width // masks[0].shape[1]
    tiles = masks[0].shape[1] // 4
    x = [part for group in groups for part in group]
    rows = [sum(part.shape[0] for part in group) for group in groups]
    return pl.pallas_call(
        functools.partial(stream_pairs_kernel, name, len(x), rows),
        in_specs=[HBM_SPEC] * 4 + [VMEM_SPEC] * len(x) + [ANY_SPEC] * len(deps),
        out_specs=[VMEM_SPEC] * len(rows),
        out_shape=[jax.ShapeDtypeStruct((size, width // 2), F32) for size in rows],
        scratch_shapes=[pltpu.VMEM((tiles, depth, 2 * blk), BF16)] + pairs_scratch(masks[0], tiles),
        compiler_params=pltpu.CompilerParams(vmem_limit_bytes=22 * MIB),
        cost_estimate=cost(2 * sum(rows) * depth * width // 2, 2 * 2 * depth * width // 4),
        name="stream_" + name,
    )(*[in_hbm(v) for v in (*masks, *weights)], *[in_vmem(part) for part in x], *deps)


def load_down_kernel(names, mask_hbm, down_hbm, *refs):
    count = len(names)
    bufs, (mask, sem, mask_sem) = refs[-3 - count : -3], refs[-3:]
    panels, depth, width = bufs[0].shape
    cols = mask.shape[1]
    blk = width // cols
    first = [quarter_of(name) * panels for name in names]
    mask_copy = pltpu.make_async_copy(mask_hbm, mask, mask_sem)

    def copy(k, p):
        rows = pl.ds(pl.multiple_of((first[k] + p) * depth, depth), depth)
        return pltpu.make_async_copy(down_hbm.at[rows], bufs[k].at[p], sem.at[k, p])

    mask_copy.start()
    for k in range(count):
        loop(panels, lambda p, k=k: copy(k, p).start())
    mask_copy.wait()
    for k in range(count):

        def keep(p, k=k):
            copy(k, p).wait()
            for j in range(cols):
                at = slice(j * blk, (j + 1) * blk)
                bufs[k][p, :, at] = bufs[k][p, :, at] * factor(mask, first[k] + p, j)

        loop(panels, keep)


def load_down(names, mask, down, deps=()):
    count = len(names)
    panels = mask.shape[0] // 4
    depth, width = down.shape
    return pl.pallas_call(
        functools.partial(load_down_kernel, names),
        in_specs=[HBM_SPEC] * 2 + [ANY_SPEC] * len(deps),
        out_specs=[VMEM_SPEC] * count,
        out_shape=[pltpu.VMEM((panels, depth // mask.shape[0], width), BF16)] * count,
        scratch_shapes=[
            pltpu.SMEM(mask.shape, mask.dtype),
            pltpu.SemaphoreType.DMA((count, panels)),
            pltpu.SemaphoreType.DMA,
        ],
        compiler_params=pltpu.CompilerParams(vmem_limit_bytes=4 * MIB),
        cost_estimate=cost(0, 2 * depth * width * count // 4),
        name="load_down",
    )(in_hbm(mask), in_hbm(down), *deps)


def held_down_kernel(tile, count, *refs):
    hidden, bufs, (mine, other, rows) = refs[:count], refs[count : 2 * count], refs[-3:]
    panels, blk, width = bufs[0].shape
    half = mine.shape[0]
    for k, part in enumerate(hidden):
        rows[:, k * panels * blk : (k + 1) * panels * blk] = part[...]

    def step(n):
        at = pl.ds(pl.multiple_of(n * tile, tile), tile)
        w = jnp.concatenate([buf[:, :, at].reshape(panels * blk, tile) for buf in bufs], axis=0)
        total = jnp.dot(rows[...], w, preferred_element_type=F32)
        mine[:, at] = total[:half]
        other[:, at] = total[half:].astype(other.dtype)

    loop(width // tile, step, unroll=2)


def held_down(hidden, bufs, dtype, tile=256, deps=()):
    panels, blk, width = bufs[0].shape
    rows = hidden[0].shape[0]
    depth = panels * blk * len(hidden)
    return pl.pallas_call(
        functools.partial(held_down_kernel, tile, len(hidden)),
        in_specs=[VMEM_SPEC] * (2 * len(hidden)) + [ANY_SPEC] * len(deps),
        out_specs=[VMEM_SPEC] * 2,
        out_shape=[
            jax.ShapeDtypeStruct((rows // 2, width), F32),
            jax.ShapeDtypeStruct((rows // 2, width), dtype),
        ],
        scratch_shapes=[pltpu.VMEM((rows, depth), BF16)],
        compiler_params=pltpu.CompilerParams(vmem_limit_bytes=4 * MIB),
        cost_estimate=cost(2 * rows * depth * width, 2 * depth * width // 2),
        name="held_down",
    )(*[in_vmem(h) for h in hidden], *[in_vmem(b) for b in bufs], *deps)


def gated_kernel(first, own, got_first, got_second, *refs):
    out = refs[-1]
    rows, width = out.shape
    gate, up = [
        own[:, at] + got_first[:, at].astype(F32) + got_second[first : first + rows, at].astype(F32)
        for at in (slice(0, width), slice(width, 2 * width))
    ]
    out[...] = (jax.nn.silu(gate) * up).astype(out.dtype)


def gated(own, got_first, got_second, first, deps=()):
    rows, width = own.shape
    return pl.pallas_call(
        functools.partial(gated_kernel, first),
        in_specs=[VMEM_SPEC] * 3 + [ANY_SPEC] * len(deps),
        out_specs=VMEM_SPEC,
        out_shape=jax.ShapeDtypeStruct((rows, width // 2), BF16),
        compiler_params=pltpu.CompilerParams(vmem_limit_bytes=8 * MIB),
        cost_estimate=cost(0, 8 * rows * width),
        name="gated",
    )(in_vmem(own), in_vmem(got_first), in_vmem(got_second), *deps)


class Exchange:
    def __init__(self, rows, cols):
        self.rows, self.cols = rows, cols

    def swap(self, value, row_bits, col_bits):
        pairs = []
        for r in range(self.rows):
            for c in range(self.cols):
                pairs.append((r * self.cols + c, (r ^ row_bits(c)) * self.cols + (c ^ col_bits)))
        return lax.ppermute(value, ("row", "col"), pairs)

    def core(self, value):
        return self.swap(value, lambda c: 0, 1)

    def near(self, value):
        return self.swap(value, lambda c: 0, 2)

    def far(self, value):
        return self.swap(value, lambda c: 0, 4)

    def first(self, value):
        return self.swap(value, lambda c: 1 + (c & 1), 0)

    def second(self, value):
        return self.swap(value, lambda c: 2 - (c & 1), 0)


def paired(tokens, gate_weight, up_weight, down_weight, gate_mask, up_mask, down_mask, swap):
    weights = (gate_weight, up_weight)
    masks = (gate_mask, up_mask)
    width = gate_weight.shape[1] // 4
    blk = tokens.shape[0]

    near = swap.near(tokens)
    far = swap.far(tokens)
    core = swap.core(tokens)
    w_last = load_pairs("last", masks, weights)
    w_first = load_pairs("first", masks, weights, deps=(w_last,))
    near = tie(near, w_first)
    far = tie(far, w_first)
    far_near = swap.near(far)
    close = (tokens, near, core, swap.core(near))
    close_last = held_pairs(close, w_last)
    got_close_last = swap.first(close_last)
    w_second = load_pairs("second", masks, weights, deps=(close_last,))
    far_near = tie(far_near, w_second)
    distant = (far, far_near, swap.core(far), swap.core(far_near))
    distant_last = held_pairs(distant, w_last, deps=(got_close_last,))
    got_distant_last = swap.first(distant_last)
    close_first = held_pairs(close, w_first, deps=(distant_last,))
    got_close_first = swap.first(close_first)
    distant_first = held_pairs(distant, w_first, deps=(close_first,))
    got_distant_first = swap.first(distant_first)
    second = held_pairs(
        distant + close, w_second, added=(got_distant_last, got_close_last), deps=(distant_first,)
    )
    second = tie(second, got_close_first)
    got_second = swap.second(second)
    distant_own, close_own = stream_pairs("own", masks, weights, (distant, close), deps=(second,))
    w_down = load_down(("own",), down_mask, down_weight, deps=(distant_own, got_distant_first))

    distant_hidden = gated(distant_own, got_distant_first, got_second, 0, deps=w_down)
    close_hidden = gated(close_own, got_close_first, got_second, 4 * blk, deps=(distant_hidden,))
    w_down += load_down(("second", "first"), down_mask, down_weight, deps=(close_hidden,))

    def gathered(hidden):
        second, first = swap.second(hidden), swap.first(hidden)
        second = tie(second, w_down[1])
        return [hidden, second, first, swap.first(second)]

    distant_hidden = gathered(distant_hidden)
    close_hidden = gathered(close_hidden)
    w_down += load_down(("last",), down_mask, down_weight, deps=(distant_hidden[1],))

    mine, other = held_down(distant_hidden, w_down, F32, deps=close_hidden)
    mine = mine + swap.core(other)
    near_sum = mine[blk:].astype(BF16)
    got_near = swap.near(near_sum)
    got_far = swap.far((mine[:blk] + got_near).astype(BF16))
    mine, other = held_down(close_hidden, w_down, F32, deps=(near_sum,))
    mine = mine + swap.core(other)
    got_near = swap.near(mine[blk:].astype(BF16))
    return (mine[:blk] + got_near + got_far).astype(BF16)


def solution(mesh):
    rows, cols = mesh.shape["row"], mesh.shape["col"]
    body = plain
    if (rows, cols) == (4, 8):
        body = functools.partial(paired, swap=Exchange(rows, cols))
    return jax.shard_map(
        body,
        mesh=mesh,
        in_specs=(
            P("col", "row"),
            P("row", "col"),
            P("row", "col"),
            P("col", "row"),
            P("row", "col"),
            P("row", "col"),
            P("col", "row"),
        ),
        out_specs=P("col", "row"),
        check_vma=False,
    )
```

time: 416 us -> 118 us (0.28)
  waiting for transfers between devices: 210 us -> 32.5 us
  local copies, waits for them, and re-layouts: 106 us -> 0.06 us
  matrix products: 74.8 us -> 0 us
  Pallas kernels: 0 us -> 61.7 us
  starting transfers between devices: 0.26 us -> 22 us
  between operations: 13.1 us -> 0.27 us
  other arithmetic: 9.08 us -> 1.06 us
    psum x1 -> x0, waiting for transfers between devices: 159 us -> none  [on_device(): summed = lax.psum(partial_sums, 'row')]
    unnamed x8 -> x2, local copies, waits for them, and re-layouts: 76.5 us -> 0.01 us
    dot_general x3 -> x0, matrix products: 74.8 us -> none  [the longest x1 29.8 us: on_device(): jnp.dot(hidden, down_kept, preferred_element_type=jnp.float32)]
    pallas_call x0 -> x22, Pallas kernels: none -> 61.7 us  [the longest x3 18.1 us: load_pairs(): pl.pallas_call(functools.partial(load_pairs_kernel, name), in_specs=[HBM_...]
    reduce_scatter x1 -> x0, waiting for transfers between devices: 50.2 us -> none  [on_device(): lax.psum_scatter(jnp.dot(hidden, down_kept, preferred_element_type=jnp.fl...]
    ppermute x0 -> x23, waiting for transfers between devices: none -> 32.5 us  [swap(): return lax.ppermute(value, ('row', 'col'), pairs)]
    mul x3 -> x0, local copies, waits for them, and re-layouts: 29.7 us -> none  [apply_blocks(): kept = shaped * mask.astype(weight.dtype)[:, None, :, None]]
    ppermute x0 -> x23, starting transfers between devices: none -> 22 us  [swap(): return lax.ppermute(value, ('row', 'col'), pairs)]
  transfers between devices with their start and end apart: 3 -> 23, of which waited for: 2 -> 12; matrix products, arithmetic and copies ran while one was open for 19% -> 0% of each run, Pallas kernels for 0% -> 45%
where the time goes in v1:
time: 118 us
  Pallas kernels  61.7 us (52%)
  waiting for transfers between devices  32.5 us (28%)
  starting transfers between devices  22 us (19%)
    ppermute x23, waiting for transfers between devices, swap(): return lax.ppermute(value, ('row', 'col'), pairs)  32.5 us
    ppermute x23, starting transfers between devices, swap(): return lax.ppermute(value, ('row', 'col'), pairs)  22 us
    pallas_call x3, Pallas kernels, load_pairs(): pl.pallas_call(functools.partial(load_pairs_kernel, name), in_specs=[HBM_...  18.1 us
    pallas_call x3, Pallas kernels, load_down(): pl.pallas_call(functools.partial(load_down_kernel, names), in_specs=[HBM_...  12.5 us
    pallas_call x5, Pallas kernels, held_pairs(): pl.pallas_call(functools.partial(held_pairs_kernel, len(x), len(added)),...  12.2 us
    pallas_call x2, Pallas kernels, held_down(): pl.pallas_call(functools.partial(held_down_kernel, tile, len(hidden)), in...  11.7 us
    pallas_call x1, Pallas kernels, stream_pairs(): pl.pallas_call(functools.partial(stream_pairs_kernel, name, len(x), rows)...  6.82 us
  transfers between devices with their start and end apart: 23, of which 12 were waited for; matrix products, arithmetic and copies ran while one was open for 0% of the time, Pallas kernels for 45%

profile of v1, /device:TPU:0, one launch (start us, length us, event | category | flops | bytes accessed | tf_op | source)
XLA Modules:
  0.0 117.6 jit_solution(7561347676391697512)
XLA Ops:
  0.0 3.0 %collective-permute-start.2 = (bf16[32,4096]{1,0:T(8,128)(2,1)}, bf16[32,4096]{1,0:T(8,128)(2,1)S(1)}, u32[]{:S(2)}, u32[]{:S(2)}) collective-permute-start(bf16[32,4096]{1,0:T(8,128)(2,1)} %refs_8_.1), channel_id=1, source_target_pairs={{0,2},{1,3},{2,0},{3,1},{4,6},{5,7},{6,4},{7,5},{8,10},{9,11},{10,... | collective-permute-start | bytes 786440 | tf_op jit(solution)/shard_map/ppermute | solution.py:373
  3.0 2.6 %collective-permute-start = (bf16[32,4096]{1,0:T(8,128)(2,1)}, bf16[32,4096]{1,0:T(8,128)(2,1)S(1)}, u32[]{:S(2)}, u32[]{:S(2)}) collective-permute-start(bf16[32,4096]{1,0:T(8,128)(2,1)} %refs_8_.1), channel_id=1, source_target_pairs={{0,4},{1,5},{2,6},{3,7},{4,0},{5,1},{6,2},{7,3},{8,12},{9,13},{10,... | collective-permute-start | bytes 786440 | tf_op jit(solution)/shard_map/ppermute | solution.py:373
  5.6 6.0 %load_last.1.refs_4_ = bf16[7,4096,256]{2,1,0:T(8,128)(2,1)S(1)} custom-call(s32[32,28]{1,0:T(8,128)} %refs_0_.11, s32[32,28]{1,0:T(8,128)} %refs_1_.7, bf16[4096,3584]{1,0:T(8,128)(2,1)} %refs_2_.7, bf16[4096,3584]{1,0:T(8,128)(2,1)} %refs_3_.7), custom_call_target="tpu_custom_call" | custom-call | bytes 14680064 | tf_op jit(solution)/shard_map/load_last/pallas_call | solution.py:182
  11.6 6.0 %load_first.1.refs_1_.refs_4_ = bf16[7,4096,256]{2,1,0:T(8,128)(2,1)S(1)} custom-call(s32[32,28]{1,0:T(8,128)} %refs_0_.11, s32[32,28]{1,0:T(8,128)} %refs_1_.7, bf16[4096,3584]{1,0:T(8,128)(2,1)} %refs_2_.7, bf16[4096,3584]{1,0:T(8,128)(2,1)} %refs_3_.7, bf16[7,4096,256]{2,1,0:T(8,128)(2,1)S(1)} %load_last.1.refs_4_), custom_call_target="tpu_custom_call" | custom-call | bytes 14680064 | tf_op jit(solution)/shard_map/load_first/pallas_call | solution.py:182
  19.2 2.1 %held_pairs.5.refs_4_ = bf16[128,1792]{1,0:T(8,128)(2,1)S(1)} custom-call(bf16[32,4096]{1,0:T(8,128)(2,1)S(1)} %copy-done, bf16[32,4096]{1,0:T(8,128)(2,1)S(1)} %tie.7.refs_1_.refs_5_.refs_9_, bf16[32,4096]{1,0:T(8,128)(2,1)S(1)} %collective-permute-done.3.refs_2_.refs_6_.refs_10_, bf16[32,4096]{1,0:T(8,128)(2,1)S(1)} %collective-permute-done.4.refs_3_.refs_7_.refs_11_, ...), custom_call_target="tpu_custom_call" | custom-call | flops 1879048192 | bytes 7340032 | tf_op jit(solution)/shard_map/held_pairs/pallas_call | solution.py:210
  21.3 1.6 %collective-permute-start.7 = (bf16[128,1792]{1,0:T(8,128)(2,1)S(1)}, bf16[128,1792]{1,0:T(8,128)(2,1)S(1)}, u32[]{:S(2)}, u32[]{:S(2)}) collective-permute-start(bf16[128,1792]{1,0:T(8,128)(2,1)S(1)} %held_pairs.5.refs_4_), channel_id=1, source_target_pairs={{0,8},{1,17},{2,10},{3,19},{4,12},{5,21},{6,14},{7,23},{8,0},{9,25... | collective-permute-start | bytes 1376264 | tf_op jit(solution)/shard_map/ppermute | solution.py:373
  22.9 6.1 %load_second.1.refs_1_.refs_8_ = bf16[7,4096,256]{2,1,0:T(8,128)(2,1)S(1)} custom-call(s32[32,28]{1,0:T(8,128)} %refs_0_.11, s32[32,28]{1,0:T(8,128)} %refs_1_.7, bf16[4096,3584]{1,0:T(8,128)(2,1)} %refs_2_.7, bf16[4096,3584]{1,0:T(8,128)(2,1)} %refs_3_.7, bf16[128,1792]{1,0:T(8,128)(2,1)S(1)} %held_pairs.5.refs_4_), custom_call_target="tpu_custom_call" | custom-call | bytes 14680064 | tf_op jit(solution)/shard_map/load_second/pallas_call | solution.py:182
  30.8 2.1 %held_pairs.6.refs_5_ = bf16[128,1792]{1,0:T(8,128)(2,1)S(1)} custom-call(bf16[32,4096]{1,0:T(8,128)(2,1)S(1)} %tie.6.refs_0_.refs_4_, bf16[32,4096]{1,0:T(8,128)(2,1)S(1)} %tie.8.refs_1_.refs_5_, bf16[32,4096]{1,0:T(8,128)(2,1)S(1)} %collective-permute-done.5.refs_2_.refs_6_, bf16[32,4096]{1,0:T(8,128)(2,1)S(1)} %collective-permute-done.6.refs_3_.refs_7_, ...), custom_call_target="tpu_custom_call" | custom-call | flops 1879048192 | bytes 7340032 | tf_op jit(solution)/shard_map/held_pairs/pallas_call | solution.py:210
  34.2 2.1 %held_pairs.7.refs_5_ = bf16[128,1792]{1,0:T(8,128)(2,1)S(1)} custom-call(bf16[32,4096]{1,0:T(8,128)(2,1)S(1)} %copy-done, bf16[32,4096]{1,0:T(8,128)(2,1)S(1)} %tie.7.refs_1_.refs_5_.refs_9_, bf16[32,4096]{1,0:T(8,128)(2,1)S(1)} %collective-permute-done.3.refs_2_.refs_6_.refs_10_, bf16[32,4096]{1,0:T(8,128)(2,1)S(1)} %collective-permute-done.4.refs_3_.refs_7_.refs_11_, ...), custom_call_target="tpu_custom_call" | custom-call | flops 1879048192 | bytes 7340032 | tf_op jit(solution)/shard_map/held_pairs/pallas_call | solution.py:210
  37.1 2.1 %held_pairs.8.refs_11_ = bf16[128,1792]{1,0:T(8,128)(2,1)S(1)} custom-call(bf16[32,4096]{1,0:T(8,128)(2,1)S(1)} %tie.6.refs_0_.refs_4_, bf16[32,4096]{1,0:T(8,128)(2,1)S(1)} %tie.8.refs_1_.refs_5_, bf16[32,4096]{1,0:T(8,128)(2,1)S(1)} %collective-permute-done.5.refs_2_.refs_6_, bf16[32,4096]{1,0:T(8,128)(2,1)S(1)} %collective-permute-done.6.refs_3_.refs_7_, ...), custom_call_target="tpu_custom_call" | custom-call | flops 1879048192 | bytes 7340032 | tf_op jit(solution)/shard_map/held_pairs/pallas_call | solution.py:210
  39.1 2.2 %collective-permute-done.8.refs_9_ = bf16[128,1792]{1,0:T(8,128)(2,1)S(1)} collective-permute-done((bf16[128,1792]{1,0:T(8,128)(2,1)S(1)}, bf16[128,1792]{1,0:T(8,128)(2,1)S(1)}, u32[]{:S(2)}, u32[]{:S(2)}) %collective-permute-start.8) | collective-permute-done | bytes 458784 | tf_op jit(solution)/shard_map/ppermute | solution.py:373
  41.4 3.9 %held_pairs.9.refs_0_ = bf16[256,1792]{1,0:T(8,128)(2,1)S(1)} custom-call(bf16[32,4096]{1,0:T(8,128)(2,1)S(1)} %tie.6.refs_0_.refs_4_, bf16[32,4096]{1,0:T(8,128)(2,1)S(1)} %tie.8.refs_1_.refs_5_, bf16[32,4096]{1,0:T(8,128)(2,1)S(1)} %collective-permute-done.5.refs_2_.refs_6_, bf16[32,4096]{1,0:T(8,128)(2,1)S(1)} %collective-permute-done.6.refs_3_.refs_7_, ...), custom_call_target="tpu_custom_call" | custom-call | flops 3758096384 | bytes 7340032 | tf_op jit(solution)/shard_map/held_pairs/pallas_call | solution.py:210
  48.4 6.8 %stream_own.1 = (f32[128,1792]{1,0:T(8,128)S(1)}, f32[128,1792]{1,0:T(8,128)S(1)}) custom-call(s32[32,28]{1,0:T(8,128)} %refs_0_.11, s32[32,28]{1,0:T(8,128)} %refs_1_.7, bf16[4096,3584]{1,0:T(8,128)(2,1)} %refs_2_.7, bf16[4096,3584]{1,0:T(8,128)(2,1)} %refs_3_.7, bf16[32,4096]{1,0:T(8,128)(2,1)S(1)} %tie.6.refs_0_.refs_4_, ...), custom_call_target="tpu_custom_call" | custom-call | flops 3758096384 | bytes 14680064 | tf_op jit(solution)/shard_map/stream_own/pallas_call | solution.py:245
  55.2 6.1 %collective-permute-done.11.refs_1_.got_first = bf16[128,1792]{1,0:T(8,128)(2,1)S(1)} collective-permute-done((bf16[128,1792]{1,0:T(8,128)(2,1)S(1)}, bf16[128,1792]{1,0:T(8,128)(2,1)S(1)}, u32[]{:S(2)}, u32[]{:S(2)}) %collective-permute-start.11) | collective-permute-done | bytes 458784 | tf_op jit(solution)/shard_map/ppermute | solution.py:373
  61.3 3.5 %load_down.3.refs_0_.refs_4_ = bf16[7,128,4096]{2,1,0:T(8,128)(2,1)S(1)} custom-call(s32[28,32]{1,0:T(8,128)} %mask_hbm.5, bf16[3584,4096]{1,0:T(8,128)(2,1)} %down_hbm.5, f32[128,1792]{1,0:T(8,128)S(1)} %get-tuple-element.14.refs_0_.own, bf16[128,1792]{1,0:T(8,128)(2,1)S(1)} %collective-permute-done.11.refs_1_.got_first), custom_call_target="tpu_custom_call" | custom-call | bytes 7340032 | tf_op jit(solution)/shard_map/load_down/pallas_call | solution.py:289
  69.3 5.6 %load_down.4 = (bf16[7,128,4096]{2,1,0:T(8,128)(2,1)S(1)}, bf16[7,128,4096]{2,1,0:T(8,128)(2,1)S(1)}) custom-call(s32[28,32]{1,0:T(8,128)} %mask_hbm.5, bf16[3584,4096]{1,0:T(8,128)(2,1)} %down_hbm.5, bf16[128,896]{1,0:T(8,128)(2,1)S(1)} %gated.3.refs_0_.refs_8_), custom_call_target="tpu_custom_call" | custom-call | bytes 14680064 | tf_op jit(solution)/shard_map/load_down/pallas_call | solution.py:289
  75.6 3.0 %collective-permute-done.15.refs_0_ = bf16[128,896]{1,0:T(8,128)(2,1)S(1)} collective-permute-done((bf16[128,896]{1,0:T(8,128)(2,1)S(1)}, bf16[128,896]{1,0:T(8,128)(2,1)S(1)}, u32[]{:S(2)}, u32[]{:S(2)}) %collective-permute-start.15) | collective-permute-done | bytes 229408 | tf_op jit(solution)/shard_map/ppermute | solution.py:373
  79.1 3.5 %load_down.5.refs_7_ = bf16[7,128,4096]{2,1,0:T(8,128)(2,1)S(1)} custom-call(s32[28,32]{1,0:T(8,128)} %mask_hbm.5, bf16[3584,4096]{1,0:T(8,128)(2,1)} %down_hbm.5, bf16[128,896]{1,0:T(8,128)(2,1)S(1)} %tie.11.refs_0_.refs_1_), custom_call_target="tpu_custom_call" | custom-call | bytes 7340032 | tf_op jit(solution)/shard_map/load_down/pallas_call | solution.py:289
  82.6 2.0 %collective-permute-done.17.refs_3_ = bf16[128,896]{1,0:T(8,128)(2,1)S(1)} collective-permute-done((bf16[128,896]{1,0:T(8,128)(2,1)S(1)}, bf16[128,896]{1,0:T(8,128)(2,1)S(1)}, u32[]{:S(2)}, u32[]{:S(2)}) %collective-permute-start.17) | collective-permute-done | bytes 229408 | tf_op jit(solution)/shard_map/ppermute | solution.py:373
  84.6 5.8 %held_down.2 = (f32[64,4096]{1,0:T(8,128)S(1)}, f32[64,4096]{1,0:T(8,128)S(1)}) custom-call(bf16[128,896]{1,0:T(8,128)(2,1)S(1)} %gated.2.refs_0_, bf16[128,896]{1,0:T(8,128)(2,1)S(1)} %tie.11.refs_0_.refs_1_, bf16[128,896]{1,0:T(8,128)(2,1)S(1)} %collective-permute-done.16.refs_2_, bf16[128,896]{1,0:T(8,128)(2,1)S(1)} %collective-permute-done.17.refs_3_, ...), custom_call_target="tpu_custom_call" | custom-call | flops 3758096384 | bytes 14680064 | tf_op jit(solution)/shard_map/held_down/pallas_call | solution.py:326
  90.6 2.6 %collective-permute-done.18 = f32[64,4096]{1,0:T(8,128)S(1)} collective-permute-done((f32[64,4096]{1,0:T(8,128)S(1)}, f32[64,4096]{1,0:T(8,128)S(1)}, u32[]{:S(2)}, u32[]{:S(2)}) %collective-permute-start.18) | collective-permute-done | bytes 1048608 | tf_op jit(solution)/shard_map/ppermute | solution.py:373
  94.8 5.8 %held_down.3 = (f32[64,4096]{1,0:T(8,128)S(1)}, f32[64,4096]{1,0:T(8,128)S(1)}) custom-call(bf16[128,896]{1,0:T(8,128)(2,1)S(1)} %gated.3.refs_0_.refs_8_, bf16[128,896]{1,0:T(8,128)(2,1)S(1)} %tie.10.refs_9_.refs_1_, bf16[128,896]{1,0:T(8,128)(2,1)S(1)} %collective-permute-done.13.refs_10_.refs_2_, ...), custom_call_target="tpu_custom_call" | custom-call | flops 3758096384 | bytes 14680064 | tf_op jit(solution)/shard_map/held_down/pallas_call | solution.py:326
  101.8 2.4 %collective-permute-start.22 = (bf16[32,4096]{1,0:T(8,128)(2,1)S(1)}, bf16[32,4096]{1,0:T(8,128)(2,1)S(1)}, u32[]{:S(2)}, u32[]{:S(2)}) collective-permute-start(bf16[32,4096]{1,0:T(8,128)(2,1)S(1)} %fusion), channel_id=1, source_target_pairs={{0,4},{1,5},{2,6},{3,7},{4,0},{5,1},{6,2},{7,3},{8,12},{9,13},{10,... | collective-permute-start | bytes 786440 | tf_op jit(solution)/shard_map/ppermute | solution.py:373
  104.8 11.4 %collective-permute-done.22 = bf16[32,4096]{1,0:T(8,128)(2,1)S(1)} collective-permute-done((bf16[32,4096]{1,0:T(8,128)(2,1)S(1)}, bf16[32,4096]{1,0:T(8,128)(2,1)S(1)}, u32[]{:S(2)}, u32[]{:S(2)}) %collective-permute-start.22) | collective-permute-done | bytes 262176 | tf_op jit(solution)/shard_map/ppermute | solution.py:373
  (52 shorter events, 19.0 us)
Async XLA Ops:
  0.0 17.6 %collective-permute-start.2 = (bf16[32,4096]{1,0:T(8,128)(2,1)}, bf16[32,4096]{1,0:T(8,128)(2,1)S(1)}, u32[]{:S(2)}, u32[]{:S(2)}) collective-permute-start(bf16[32,4096]{1,0:T(8,128)(2,1)} %refs_8_.1), channel_id=1, source_target_pairs={{0,2},{1,3},{2,0},{3,1},{4,6},{5,7},{6,4},{7,5},{8,10},{9,11},{10,... | collective-permute-start | bytes 786440 | tf_op jit(solution)/shard_map/ppermute | solution.py:373
  3.0 15.5 %collective-permute-start.3 = (bf16[32,4096]{1,0:T(8,128)(2,1)}, bf16[32,4096]{1,0:T(8,128)(2,1)S(1)}, u32[]{:S(2)}, u32[]{:S(2)}) collective-permute-start(bf16[32,4096]{1,0:T(8,128)(2,1)} %refs_8_.1), channel_id=1, source_target_pairs={{0,1},{1,0},{2,3},{3,2},{4,5},{5,4},{6,7},{7,6},{8,9},{9,8},{10,11... | collective-permute-start | bytes 786440 | tf_op jit(solution)/shard_map/ppermute | solution.py:373
  3.0 15.5 %collective-permute-start = (bf16[32,4096]{1,0:T(8,128)(2,1)}, bf16[32,4096]{1,0:T(8,128)(2,1)S(1)}, u32[]{:S(2)}, u32[]{:S(2)}) collective-permute-start(bf16[32,4096]{1,0:T(8,128)(2,1)} %refs_8_.1), channel_id=1, source_target_pairs={{0,4},{1,5},{2,6},{3,7},{4,0},{5,1},{6,2},{7,3},{8,12},{9,13},{10,... | collective-permute-start | bytes 786440 | tf_op jit(solution)/shard_map/ppermute | solution.py:373
  17.6 1.6 %copy-start = (bf16[32,4096]{1,0:T(8,128)(2,1)S(1)}, bf16[32,4096]{1,0:T(8,128)(2,1)}, u32[]{:S(2)}) copy-start(bf16[32,4096]{1,0:T(8,128)(2,1)} %refs_8_.1) | copy-start | bytes 786436
  17.6 1.6 %collective-permute-start.4 = (bf16[32,4096]{1,0:T(8,128)(2,1)S(1)}, bf16[32,4096]{1,0:T(8,128)(2,1)S(1)}, u32[]{:S(2)}, u32[]{:S(2)}) collective-permute-start(bf16[32,4096]{1,0:T(8,128)(2,1)S(1)} %tie.7.refs_1_.refs_5_.refs_9_), channel_id=1, source_target_pairs={{0,1},{1,0},{2,3},{3,2},{4,5},{5,4},{6,7},{7,6},{8,9},{9,8},{10,11... | collective-permute-start | bytes 786440 | tf_op jit(solution)/shard_map/ppermute | solution.py:373
  18.5 10.5 %collective-permute-start.1 = (bf16[32,4096]{1,0:T(8,128)(2,1)S(1)}, bf16[32,4096]{1,0:T(8,128)(2,1)S(1)}, u32[]{:S(2)}, u32[]{:S(2)}) collective-permute-start(bf16[32,4096]{1,0:T(8,128)(2,1)S(1)} %tie.6.refs_0_.refs_4_), channel_id=1, source_target_pairs={{0,2},{1,3},{2,0},{3,1},{4,6},{5,7},{6,4},{7,5},{8,10},{9,11},{10,... | collective-permute-start | bytes 786440 | tf_op jit(solution)/shard_map/ppermute | solution.py:373
  21.3 9.5 %collective-permute-start.7 = (bf16[128,1792]{1,0:T(8,128)(2,1)S(1)}, bf16[128,1792]{1,0:T(8,128)(2,1)S(1)}, u32[]{:S(2)}, u32[]{:S(2)}) collective-permute-start(bf16[128,1792]{1,0:T(8,128)(2,1)S(1)} %held_pairs.5.refs_4_), channel_id=1, source_target_pairs={{0,8},{1,17},{2,10},{3,19},{4,12},{5,21},{6,14},{7,23},{8,0},{9,25... | collective-permute-start | bytes 1376264 | tf_op jit(solution)/shard_map/ppermute | solution.py:373
  22.9 6.7 %collective-permute-start.5 = (bf16[32,4096]{1,0:T(8,128)(2,1)S(1)}, bf16[32,4096]{1,0:T(8,128)(2,1)S(1)}, u32[]{:S(2)}, u32[]{:S(2)}) collective-permute-start(bf16[32,4096]{1,0:T(8,128)(2,1)S(1)} %tie.6.refs_0_.refs_4_), channel_id=1, source_target_pairs={{0,1},{1,0},{2,3},{3,2},{4,5},{5,4},{6,7},{7,6},{8,9},{9,8},{10,11... | collective-permute-start | bytes 786440 | tf_op jit(solution)/shard_map/ppermute | solution.py:373
  29.0 1.7 %collective-permute-start.6 = (bf16[32,4096]{1,0:T(8,128)(2,1)S(1)}, bf16[32,4096]{1,0:T(8,128)(2,1)S(1)}, u32[]{:S(2)}, u32[]{:S(2)}) collective-permute-start(bf16[32,4096]{1,0:T(8,128)(2,1)S(1)} %tie.8.refs_1_.refs_5_), channel_id=1, source_target_pairs={{0,1},{1,0},{2,3},{3,2},{4,5},{5,4},{6,7},{7,6},{8,9},{9,8},{10,11... | collective-permute-start | bytes 786440 | tf_op jit(solution)/shard_map/ppermute | solution.py:373
  32.8 8.5 %collective-permute-start.8 = (bf16[128,1792]{1,0:T(8,128)(2,1)S(1)}, bf16[128,1792]{1,0:T(8,128)(2,1)S(1)}, u32[]{:S(2)}, u32[]{:S(2)}) collective-permute-start(bf16[128,1792]{1,0:T(8,128)(2,1)S(1)} %held_pairs.6.refs_5_), channel_id=1, source_target_pairs={{0,8},{1,17},{2,10},{3,19},{4,12},{5,21},{6,14},{7,23},{8,0},{9,25... | collective-permute-start | bytes 1376264 | tf_op jit(solution)/shard_map/ppermute | solution.py:373
  36.3 10.0 %collective-permute-start.9 = (bf16[128,1792]{1,0:T(8,128)(2,1)S(1)}, bf16[128,1792]{1,0:T(8,128)(2,1)S(1)}, u32[]{:S(2)}, u32[]{:S(2)}) collective-permute-start(bf16[128,1792]{1,0:T(8,128)(2,1)S(1)} %held_pairs.7.refs_5_), channel_id=1, source_target_pairs={{0,8},{1,17},{2,10},{3,19},{4,12},{5,21},{6,14},{7,23},{8,0},{9,25... | collective-permute-start | bytes 1376264 | tf_op jit(solution)/shard_map/ppermute | solution.py:373
  46.3 18.5 %collective-permute-start.10 = (bf16[256,1792]{1,0:T(8,128)(2,1)S(1)}, bf16[256,1792]{1,0:T(8,128)(2,1)S(1)}, u32[]{:S(2)}, u32[]{:S(2)}) collective-permute-start(bf16[256,1792]{1,0:T(8,128)(2,1)S(1)} %tie.9.refs_12_), channel_id=1, source_target_pairs={{0,16},{1,9},{2,18},{3,11},{4,20},{5,13},{6,22},{7,15},{8,24},{9,1... | collective-permute-start | bytes 2752520 | tf_op jit(solution)/shard_map/ppermute | solution.py:373
  47.8 13.5 %collective-permute-start.11 = (bf16[128,1792]{1,0:T(8,128)(2,1)S(1)}, bf16[128,1792]{1,0:T(8,128)(2,1)S(1)}, u32[]{:S(2)}, u32[]{:S(2)}) collective-permute-start(bf16[128,1792]{1,0:T(8,128)(2,1)S(1)} %held_pairs.8.refs_11_), channel_id=1, source_target_pairs={{0,8},{1,17},{2,10},{3,19},{4,12},{5,21},{6,14},{7,23},{8,0},{9,25... | collective-permute-start | bytes 1376264 | tf_op jit(solution)/shard_map/ppermute | solution.py:373
  65.2 9.7 %collective-permute-start.12 = (bf16[128,896]{1,0:T(8,128)(2,1)S(1)}, bf16[128,896]{1,0:T(8,128)(2,1)S(1)}, u32[]{:S(2)}, u32[]{:S(2)}) collective-permute-start(bf16[128,896]{1,0:T(8,128)(2,1)S(1)} %gated.3.refs_0_.refs_8_), channel_id=1, source_target_pairs={{0,16},{1,9},{2,18},{3,11},{4,20},{5,13},{6,22},{7,15},{8,24},{9,1... | collective-permute-start | bytes 688136 | tf_op jit(solution)/shard_map/ppermute | solution.py:373
  65.7 12.9 %collective-permute-start.15 = (bf16[128,896]{1,0:T(8,128)(2,1)S(1)}, bf16[128,896]{1,0:T(8,128)(2,1)S(1)}, u32[]{:S(2)}, u32[]{:S(2)}) collective-permute-start(bf16[128,896]{1,0:T(8,128)(2,1)S(1)} %gated.2.refs_0_), channel_id=1, source_target_pairs={{0,16},{1,9},{2,18},{3,11},{4,20},{5,13},{6,22},{7,15},{8,24},{9,1... | collective-permute-start | bytes 688136 | tf_op jit(solution)/shard_map/ppermute | solution.py:373
  67.2 15.3 %collective-permute-start.13 = (bf16[128,896]{1,0:T(8,128)(2,1)S(1)}, bf16[128,896]{1,0:T(8,128)(2,1)S(1)}, u32[]{:S(2)}, u32[]{:S(2)}) collective-permute-start(bf16[128,896]{1,0:T(8,128)(2,1)S(1)} %gated.3.refs_0_.refs_8_), channel_id=1, source_target_pairs={{0,8},{1,17},{2,10},{3,19},{4,12},{5,21},{6,14},{7,23},{8,0},{9,25... | collective-permute-start | bytes 688136 | tf_op jit(solution)/shard_map/ppermute | solution.py:373
  67.8 14.8 %collective-permute-start.16 = (bf16[128,896]{1,0:T(8,128)(2,1)S(1)}, bf16[128,896]{1,0:T(8,128)(2,1)S(1)}, u32[]{:S(2)}, u32[]{:S(2)}) collective-permute-start(bf16[128,896]{1,0:T(8,128)(2,1)S(1)} %gated.2.refs_0_), channel_id=1, source_target_pairs={{0,8},{1,17},{2,10},{3,19},{4,12},{5,21},{6,14},{7,23},{8,0},{9,25... | collective-permute-start | bytes 688136 | tf_op jit(solution)/shard_map/ppermute | solution.py:373
  74.9 7.7 %collective-permute-start.14 = (bf16[128,896]{1,0:T(8,128)(2,1)S(1)}, bf16[128,896]{1,0:T(8,128)(2,1)S(1)}, u32[]{:S(2)}, u32[]{:S(2)}) collective-permute-start(bf16[128,896]{1,0:T(8,128)(2,1)S(1)} %tie.10.refs_9_.refs_1_), channel_id=1, source_target_pairs={{0,8},{1,17},{2,10},{3,19},{4,12},{5,21},{6,14},{7,23},{8,0},{9,25... | collective-permute-start | bytes 688136 | tf_op jit(solution)/shard_map/ppermute | solution.py:373
  78.6 6.0 %collective-permute-start.17 = (bf16[128,896]{1,0:T(8,128)(2,1)S(1)}, bf16[128,896]{1,0:T(8,128)(2,1)S(1)}, u32[]{:S(2)}, u32[]{:S(2)}) collective-permute-start(bf16[128,896]{1,0:T(8,128)(2,1)S(1)} %tie.11.refs_0_.refs_1_), channel_id=1, source_target_pairs={{0,8},{1,17},{2,10},{3,19},{4,12},{5,21},{6,14},{7,23},{8,0},{9,25... | collective-permute-start | bytes 688136 | tf_op jit(solution)/shard_map/ppermute | solution.py:373
  90.5 2.7 %collective-permute-start.18 = (f32[64,4096]{1,0:T(8,128)S(1)}, f32[64,4096]{1,0:T(8,128)S(1)}, u32[]{:S(2)}, u32[]{:S(2)}) collective-permute-start(f32[64,4096]{1,0:T(8,128)S(1)} %get-tuple-element.18), channel_id=1, source_target_pairs={{0,1},{1,0},{2,3},{3,2},{4,5},{5,4},{6,7},{7,6},{8,9},{9,8},{10,11... | collective-permute-start | bytes 3145736 | tf_op jit(solution)/shard_map/ppermute | solution.py:373
  93.4 8.4 %collective-permute-start.21 = (bf16[32,4096]{1,0:T(8,128)(2,1)S(1)}, bf16[32,4096]{1,0:T(8,128)(2,1)S(1)}, u32[]{:S(2)}, u32[]{:S(2)}) collective-permute-start(bf16[32,4096]{1,0:T(8,128)(2,1)S(1)} %slice.33.refs_8_), channel_id=1, source_target_pairs={{0,2},{1,3},{2,0},{3,1},{4,6},{5,7},{6,4},{7,5},{8,10},{9,11},{10,... | collective-permute-start | bytes 786440 | tf_op jit(solution)/shard_map/ppermute | solution.py:373
  100.6 3.6 %collective-permute-start.19 = (f32[64,4096]{1,0:T(8,128)S(1)}, f32[64,4096]{1,0:T(8,128)S(1)}, u32[]{:S(2)}, u32[]{:S(2)}) collective-permute-start(f32[64,4096]{1,0:T(8,128)S(1)} %get-tuple-element.20), channel_id=1, source_target_pairs={{0,1},{1,0},{2,3},{3,2},{4,5},{5,4},{6,7},{7,6},{8,9},{9,8},{10,11... | collective-permute-start | bytes 3145736 | tf_op jit(solution)/shard_map/ppermute | solution.py:373
  101.8 14.3 %collective-permute-start.22 = (bf16[32,4096]{1,0:T(8,128)(2,1)S(1)}, bf16[32,4096]{1,0:T(8,128)(2,1)S(1)}, u32[]{:S(2)}, u32[]{:S(2)}) collective-permute-start(bf16[32,4096]{1,0:T(8,128)(2,1)S(1)} %fusion), channel_id=1, source_target_pairs={{0,4},{1,5},{2,6},{3,7},{4,0},{5,1},{6,2},{7,3},{8,12},{9,13},{10,... | collective-permute-start | bytes 786440 | tf_op jit(solution)/shard_map/ppermute | solution.py:373
  104.4 12.4 %collective-permute-start.20 = (bf16[32,4096]{1,0:T(8,128)(2,1)S(1)}, bf16[32,4096]{1,0:T(8,128)(2,1)S(1)}, u32[]{:S(2)}, u32[]{:S(2)}) collective-permute-start(bf16[32,4096]{1,0:T(8,128)(2,1)S(1)} %slice.32), channel_id=1, source_target_pairs={{0,2},{1,3},{2,0},{3,1},{4,6},{5,7},{6,4},{7,5},{8,10},{9,11},{10,... | collective-permute-start | bytes 786440 | tf_op jit(solution)/shard_map/ppermute | solution.py:373

commit v2 on v1

--- a/solution.py
+++ b/solution.py
@@ -152,14 +152,6 @@
         out[:, pl.ds(column, blk)] = value[:, t * blk : (t + 1) * blk].astype(out.dtype)
 
 
-def get_pair(got, tile, blk):
-    half = got[0].shape[1] // 2
-    columns = [pl.ds(pl.multiple_of(t * half + tile * blk, blk), blk) for t in range(2)]
-    return jnp.concatenate(
-        [jnp.concatenate([part[:, at].astype(F32) for at in columns], axis=1) for part in got], axis=0
-    )
-
-
 def load_pairs_kernel(name, *refs):
     buf, *held_masks, sem, mask_sem = refs[-5:]
     pairs = Pairs(quarter_of(name), refs[:2], refs[2:4], buf, held_masks, sem, mask_sem)
@@ -191,31 +183,28 @@
     )(*[in_hbm(v) for v in (*masks, *weights)], *deps)
 
 
-def held_pairs_kernel(count, added, *refs):
-    x, buf, got, out = refs[:count], refs[count], refs[count + 1 : count + 1 + added], refs[-1]
+def held_pairs_kernel(count, *refs):
+    x, buf, out = refs[:count], refs[count], refs[-1]
 
     def step(tile):
         rows = jnp.concatenate([part[...] for part in x], axis=0)
-        value = jnp.dot(rows, buf[tile], preferred_element_type=F32)
-        if added:
-            value = value + get_pair(got, tile, buf.shape[2] // 2)
-        put_pair(out, tile, value)
+        put_pair(out, tile, jnp.dot(rows, buf[tile], preferred_element_type=F32))
 
     loop(buf.shape[0], step, unroll=buf.shape[0])
 
 
-def held_pairs(x, buf, added=(), deps=()):
+def held_pairs(x, buf, deps=()):
     tiles, depth, wide = buf.shape
     rows = sum(part.shape[0] for part in x)
     return pl.pallas_call(
-        functools.partial(held_pairs_kernel, len(x), len(added)),
-        in_specs=[VMEM_SPEC] * (len(x) + 1 + len(added)) + [ANY_SPEC] * len(deps),
+        functools.partial(held_pairs_kernel, len(x)),
+        in_specs=[VMEM_SPEC] * (len(x) + 1) + [ANY_SPEC] * len(deps),
         out_specs=VMEM_SPEC,
         out_shape=jax.ShapeDtypeStruct((rows, tiles * wide), BF16),
         compiler_params=pltpu.CompilerParams(vmem_limit_bytes=4 * MIB),
         cost_estimate=cost(2 * rows * depth * tiles * wide, 2 * tiles * depth * wide // 2),
         name="held_pairs",
-    )(*[in_vmem(part) for part in x], in_vmem(buf), *[in_vmem(part) for part in added], *deps)
+    )(*[in_vmem(part) for part in x], in_vmem(buf), *deps)
 
 
 def stream_pairs_kernel(name, count, rows, *refs):
@@ -302,40 +291,61 @@
     )(in_hbm(mask), in_hbm(down), *deps)
 
 
-def held_down_kernel(tile, count, *refs):
-    hidden, bufs, (mine, other, rows) = refs[:count], refs[count : 2 * count], refs[-3:]
+def down_kernel(count, adds, blocks, tile, *refs):
+    hidden, bufs, total = refs[:count], refs[count : 2 * count], refs[2 * count]
+    outs, rows = refs[-1 - blocks : -1], refs[-1]
     panels, blk, width = bufs[0].shape
-    half = mine.shape[0]
+    depth = panels * blk
     for k, part in enumerate(hidden):
-        rows[:, k * panels * blk : (k + 1) * panels * blk] = part[...]
+        rows[:, k * depth : (k + 1) * depth] = part[...]
 
     def step(n):
         at = pl.ds(pl.multiple_of(n * tile, tile), tile)
-        w = jnp.concatenate([buf[:, :, at].reshape(panels * blk, tile) for buf in bufs], axis=0)
-        total = jnp.dot(rows[...], w, preferred_element_type=F32)
-        mine[:, at] = total[:half]
-        other[:, at] = total[half:].astype(other.dtype)
+        w = jnp.concatenate([buf[:, :, at].reshape(depth, tile) for buf in bufs], axis=0)
+        value = jnp.dot(rows[...], w, preferred_element_type=F32)
+        if adds:
+            value = value + total[:, at]
+        size = value.shape[0] // blocks
+        for k, out in enumerate(outs):
+            out[:, at] = value[k * size : (k + 1) * size]
 
     loop(width // tile, step, unroll=2)
 
 
-def held_down(hidden, bufs, dtype, tile=256, deps=()):
+def down(hidden, bufs, total=(), blocks=1, tile=512, deps=()):
     panels, blk, width = bufs[0].shape
-    rows = hidden[0].shape[0]
-    depth = panels * blk * len(hidden)
-    return pl.pallas_call(
-        functools.partial(held_down_kernel, tile, len(hidden)),
-        in_specs=[VMEM_SPEC] * (2 * len(hidden)) + [ANY_SPEC] * len(deps),
-        out_specs=[VMEM_SPEC] * 2,
-        out_shape=[
-            jax.ShapeDtypeStruct((rows // 2, width), F32),
-            jax.ShapeDtypeStruct((rows // 2, width), dtype),
-        ],
+    rows, depth, count = hidden[0].shape[0], len(hidden) * panels * blk, len(hidden)
+    return pl.pallas_call(
+        functools.partial(down_kernel, count, len(total), blocks, tile),
+        in_specs=[VMEM_SPEC] * (2 * count + len(total)) + [ANY_SPEC] * len(deps),
+        out_specs=[VMEM_SPEC] * blocks,
+        out_shape=[jax.ShapeDtypeStruct((rows // blocks, width), F32)] * blocks,
         scratch_shapes=[pltpu.VMEM((rows, depth), BF16)],
         compiler_params=pltpu.CompilerParams(vmem_limit_bytes=4 * MIB),
-        cost_estimate=cost(2 * rows * depth * width, 2 * depth * width // 2),
-        name="held_down",
-    )(*[in_vmem(h) for h in hidden], *[in_vmem(b) for b in bufs], *deps)
+        cost_estimate=cost(2 * rows * depth * width, 2 * depth * width),
+        name="down",
+    )(*[in_vmem(v) for v in (*hidden, *bufs, *total)], *deps)
+
+
+def added_kernel(count, *refs):
+    base, parts, out = refs[0], refs[1 : 1 + count], refs[-1]
+    first = 0
+    for part in parts:
+        at = slice(first, first + part.shape[0])
+        out[at] = (base[at] + part[...].astype(F32)).astype(out.dtype)
+        first += part.shape[0]
+
+
+def added(base, parts, deps=()):
+    return pl.pallas_call(
+        functools.partial(added_kernel, len(parts)),
+        in_specs=[VMEM_SPEC] * (1 + len(parts)) + [ANY_SPEC] * len(deps),
+        out_specs=VMEM_SPEC,
+        out_shape=jax.ShapeDtypeStruct(base.shape, BF16),
+        compiler_params=pltpu.CompilerParams(vmem_limit_bytes=4 * MIB),
+        cost_estimate=cost(0, 8 * base.size),
+        name="added",
+    )(*[in_vmem(v) for v in (base, *parts)], *deps)
 
 
 def gated_kernel(first, own, got_first, got_second, *refs):
@@ -380,6 +390,9 @@
 
     def far(self, value):
         return self.swap(value, lambda c: 0, 4)
+
+    def diagonal(self, value):
+        return self.swap(value, lambda c: 0, 6)
 
     def first(self, value):
         return self.swap(value, lambda c: 1 + (c & 1), 0)
@@ -405,45 +418,47 @@
     close = (tokens, near, core, swap.core(near))
     close_last = held_pairs(close, w_last)
     got_close_last = swap.first(close_last)
-    w_second = load_pairs("second", masks, weights, deps=(close_last,))
-    far_near = tie(far_near, w_second)
+    close_first = held_pairs(close, w_first, deps=(close_last,))
+    got_close_first = swap.first(close_first)
+    far_near = tie(far_near, close_first)
     distant = (far, far_near, swap.core(far), swap.core(far_near))
-    distant_last = held_pairs(distant, w_last, deps=(got_close_last,))
+    distant_last = tie(held_pairs(distant, w_last), got_close_last)
     got_distant_last = swap.first(distant_last)
-    close_first = held_pairs(close, w_first, deps=(distant_last,))
-    got_close_first = swap.first(close_first)
-    distant_first = held_pairs(distant, w_first, deps=(close_first,))
+    (second,) = stream_pairs(
+        "second", masks, weights, (distant + close,), deps=(distant_last, close_first)
+    )
+    second = added(second, (got_distant_last, got_close_last), deps=(got_close_first,))
+    got_second = swap.second(second)
+    distant_first = held_pairs(distant, w_first, deps=(second,))
     got_distant_first = swap.first(distant_first)
-    second = held_pairs(
-        distant + close, w_second, added=(got_distant_last, got_close_last), deps=(distant_first,)
-    )
-    second = tie(second, got_close_first)
-    got_second = swap.second(second)
-    distant_own, close_own = stream_pairs("own", masks, weights, (distant, close), deps=(second,))
-    w_down = load_down(("own",), down_mask, down_weight, deps=(distant_own, got_distant_first))
-
-    distant_hidden = gated(distant_own, got_distant_first, got_second, 0, deps=w_down)
-    close_hidden = gated(close_own, got_close_first, got_second, 4 * blk, deps=(distant_hidden,))
-    w_down += load_down(("second", "first"), down_mask, down_weight, deps=(close_hidden,))
-
-    def gathered(hidden):
-        second, first = swap.second(hidden), swap.first(hidden)
-        second = tie(second, w_down[1])
-        return [hidden, second, first, swap.first(second)]
-
-    distant_hidden = gathered(distant_hidden)
-    close_hidden = gathered(close_hidden)
-    w_down += load_down(("last",), down_mask, down_weight, deps=(distant_hidden[1],))
-
-    mine, other = held_down(distant_hidden, w_down, F32, deps=close_hidden)
+    distant_own, close_own = stream_pairs("own", masks, weights, (distant, close), deps=(distant_first,))
+
+    source = (down_mask, down_weight)
+    down_own, down_second = load_down(("own", "second"), *source, deps=(distant_own,))
+    distant = gated(distant_own, got_distant_first, got_second, 0, deps=(down_own,))
+    close = gated(close_own, got_close_first, got_second, 4 * blk, deps=(distant,))
+    second, first = swap.second(distant), swap.first(distant)
+    down_first, down_last = load_down(("first", "last"), *source, deps=(close,))
+    second = tie(second, down_last)
+    last = swap.first(second)
+    close = tie(close, second)
+    close_second, close_first = swap.second(close), swap.first(close)
+    total = down((distant, second, first), (down_own, down_second, down_first))
+    mine, other = down((last,), (down_last,), total, blocks=2)
+    other = tie(other, close_second, close_first)
+
     mine = mine + swap.core(other)
-    near_sum = mine[blk:].astype(BF16)
-    got_near = swap.near(near_sum)
-    got_far = swap.far((mine[:blk] + got_near).astype(BF16))
-    mine, other = held_down(close_hidden, w_down, F32, deps=(near_sum,))
-    mine = mine + swap.core(other)
-    got_near = swap.near(mine[blk:].astype(BF16))
-    return (mine[:blk] + got_near + got_far).astype(BF16)
+    total = down((close,), (down_own,), deps=(other,))
+    close_second = tie(close_second, *total)
+    close_last = swap.first(close_second)
+    near_rows, far_rows = mine[blk:].astype(BF16), mine[:blk]
+    got_near = swap.near(near_rows)
+    total = down((close_second, close_first), (down_second, down_first), total, deps=(near_rows,))
+    far_rows = (far_rows + got_near).astype(BF16)
+    got_far = swap.far(far_rows)
+    mine, other = down((close_last,), (down_last,), total, blocks=2)
+    mine = mine + swap.core(tie(other, far_rows))
+    return (mine[:blk] + swap.near(mine[blk:].astype(BF16)) + got_far).astype(BF16)
 
 
 def solution(mesh):

time: 118 us -> 106 us (0.90)
  waiting for transfers between devices: 32.5 us -> 20.9 us
  Pallas kernels: 61.7 us -> 58.1 us
  starting transfers between devices: 22 us -> 24.8 us
    ppermute x23, waiting for transfers between devices: 32.5 us -> 20.9 us  [swap(): return lax.ppermute(value, ('row', 'col'), pairs)]
    pallas_call x1 -> x2, Pallas kernels: 6.82 us -> 13.7 us  [stream_pairs(): pl.pallas_call(functools.partial(stream_pairs_kernel, name, len(x), rows)...]
    pallas_call x3 -> x2, Pallas kernels: 18.1 us -> 12 us  [load_pairs(): pl.pallas_call(functools.partial(load_pairs_kernel, name), in_specs=[HBM_...]
    pallas_call x7 -> x10, Pallas kernels: 23.9 us -> 20.5 us  [the longest x5 12.1 us: down(): pl.pallas_call(functools.partial(down_kernel, count, len(total), blocks,...]
    ppermute x23, starting transfers between devices: 22 us -> 24.8 us  [swap(): return lax.ppermute(value, ('row', 'col'), pairs)]
    pallas_call x3 -> x2, Pallas kernels: 12.5 us -> 11.5 us  [load_down(): pl.pallas_call(functools.partial(load_down_kernel, names), in_specs=[HBM_...]
  transfers between devices with their start and end apart: 23 -> 23, of which waited for: 12 -> 12; matrix products, arithmetic and copies ran while one was open for 0% -> 0% of each run, Pallas kernels for 45% -> 55%
where the time goes in v2:
time: 106 us; the launch traced here: 105 us
  Pallas kernels  58.1 us (55%)
  starting transfers between devices  24.8 us (23%)
  waiting for transfers between devices  20.9 us (20%)
    ppermute x23, starting transfers between devices, swap(): return lax.ppermute(value, ('row', 'col'), pairs)  24.8 us
    ppermute x23, waiting for transfers between devices, swap(): return lax.ppermute(value, ('row', 'col'), pairs)  20.9 us
    pallas_call x2, Pallas kernels, stream_pairs(): pl.pallas_call(functools.partial(stream_pairs_kernel, name, len(x), rows)...  13.7 us
    pallas_call x5, Pallas kernels, down(): pl.pallas_call(functools.partial(down_kernel, count, len(total), blocks,...  12.1 us
    pallas_call x2, Pallas kernels, load_pairs(): pl.pallas_call(functools.partial(load_pairs_kernel, name), in_specs=[HBM_...  12 us
    pallas_call x2, Pallas kernels, load_down(): pl.pallas_call(functools.partial(load_down_kernel, names), in_specs=[HBM_...  11.5 us
    pallas_call x4, Pallas kernels, held_pairs(): pl.pallas_call(functools.partial(held_pairs_kernel, len(x)), in_specs=[VM...  8.25 us
  transfers between devices with their start and end apart: 23, of which 12 were waited for; matrix products, arithmetic and copies ran while one was open for 0% of the time, Pallas kernels for 55%

profile of v2, /device:TPU:0, one launch (start us, length us, event | category | flops | bytes accessed | tf_op | source)
XLA Modules:
  0.0 105.2 jit_solution(14874820405347534407)
XLA Ops:
  0.0 3.0 %collective-permute-start.2 = (bf16[32,4096]{1,0:T(8,128)(2,1)}, bf16[32,4096]{1,0:T(8,128)(2,1)S(1)}, u32[]{:S(2)}, u32[]{:S(2)}) collective-permute-start(bf16[32,4096]{1,0:T(8,128)(2,1)} %refs_8_.3), channel_id=1, source_target_pairs={{0,2},{1,3},{2,0},{3,1},{4,6},{5,7},{6,4},{7,5},{8,10},{9,11},{10,... | collective-permute-start | bytes 786440 | tf_op jit(solution)/shard_map/ppermute | solution.py:383
  3.0 2.6 %collective-permute-start = (bf16[32,4096]{1,0:T(8,128)(2,1)}, bf16[32,4096]{1,0:T(8,128)(2,1)S(1)}, u32[]{:S(2)}, u32[]{:S(2)}) collective-permute-start(bf16[32,4096]{1,0:T(8,128)(2,1)} %refs_8_.3), channel_id=1, source_target_pairs={{0,4},{1,5},{2,6},{3,7},{4,0},{5,1},{6,2},{7,3},{8,12},{9,13},{10,... | collective-permute-start | bytes 786440 | tf_op jit(solution)/shard_map/ppermute | solution.py:383
  5.6 6.0 %load_last.1.refs_4_ = bf16[7,4096,256]{2,1,0:T(8,128)(2,1)S(1)} custom-call(s32[32,28]{1,0:T(8,128)} %refs_0_.11, s32[32,28]{1,0:T(8,128)} %refs_1_.7, bf16[4096,3584]{1,0:T(8,128)(2,1)} %refs_2_.7, bf16[4096,3584]{1,0:T(8,128)(2,1)} %refs_3_.7), custom_call_target="tpu_custom_call" | custom-call | bytes 14680064 | tf_op jit(solution)/shard_map/load_last/pallas_call | solution.py:174
  11.6 6.0 %load_first.1.refs_1_.refs_4_ = bf16[7,4096,256]{2,1,0:T(8,128)(2,1)S(1)} custom-call(s32[32,28]{1,0:T(8,128)} %refs_0_.11, s32[32,28]{1,0:T(8,128)} %refs_1_.7, bf16[4096,3584]{1,0:T(8,128)(2,1)} %refs_2_.7, bf16[4096,3584]{1,0:T(8,128)(2,1)} %refs_3_.7, bf16[7,4096,256]{2,1,0:T(8,128)(2,1)S(1)} %load_last.1.refs_4_), custom_call_target="tpu_custom_call" | custom-call | bytes 14680064 | tf_op jit(solution)/shard_map/load_first/pallas_call | solution.py:174
  19.2 2.1 %held_pairs.4.refs_5_ = bf16[128,1792]{1,0:T(8,128)(2,1)S(1)} custom-call(bf16[32,4096]{1,0:T(8,128)(2,1)S(1)} %copy-done, bf16[32,4096]{1,0:T(8,128)(2,1)S(1)} %tie.10.refs_1_.refs_9_, bf16[32,4096]{1,0:T(8,128)(2,1)S(1)} %collective-permute-done.3.refs_2_.refs_10_, bf16[32,4096]{1,0:T(8,128)(2,1)S(1)} %collective-permute-done.4.refs_3_.refs_11_, ...), custom_call_target="tpu_custom_call" | custom-call | flops 1879048192 | bytes 7340032 | tf_op jit(solution)/shard_map/held_pairs/pallas_call | solution.py:199
  22.9 2.1 %held_pairs.5.refs_1_.refs_13_ = bf16[128,1792]{1,0:T(8,128)(2,1)S(1)} custom-call(bf16[32,4096]{1,0:T(8,128)(2,1)S(1)} %copy-done, bf16[32,4096]{1,0:T(8,128)(2,1)S(1)} %tie.10.refs_1_.refs_9_, bf16[32,4096]{1,0:T(8,128)(2,1)S(1)} %collective-permute-done.3.refs_2_.refs_10_, bf16[32,4096]{1,0:T(8,128)(2,1)S(1)} %collective-permute-done.4.refs_3_.refs_11_, ...), custom_call_target="tpu_custom_call" | custom-call | flops 1879048192 | bytes 7340032 | tf_op jit(solution)/shard_map/held_pairs/pallas_call | solution.py:199
  28.0 2.1 %held_pairs.6.refs_0_ = bf16[128,1792]{1,0:T(8,128)(2,1)S(1)} custom-call(bf16[32,4096]{1,0:T(8,128)(2,1)S(1)} %tie.9.refs_0_.refs_4_, bf16[32,4096]{1,0:T(8,128)(2,1)S(1)} %tie.11.refs_1_.refs_5_, bf16[32,4096]{1,0:T(8,128)(2,1)S(1)} %collective-permute-done.5.refs_2_.refs_6_, bf16[32,4096]{1,0:T(8,128)(2,1)S(1)} %collective-permute-done.6.refs_3_.refs_7_, ...), custom_call_target="tpu_custom_call" | custom-call | flops 1879048192 | bytes 7340032 | tf_op jit(solution)/shard_map/held_pairs/pallas_call | solution.py:199
  30.1 1.6 %collective-permute-start.8 = (bf16[128,1792]{1,0:T(8,128)(2,1)S(1)}, bf16[128,1792]{1,0:T(8,128)(2,1)S(1)}, u32[]{:S(2)}, u32[]{:S(2)}) collective-permute-start(bf16[128,1792]{1,0:T(8,128)(2,1)S(1)} %tie.12.refs_12_), channel_id=1, source_target_pairs={{0,8},{1,17},{2,10},{3,19},{4,12},{5,21},{6,14},{7,23},{8,0},{9,25... | collective-permute-start | bytes 1376264 | tf_op jit(solution)/shard_map/ppermute | solution.py:383
  31.6 6.9 %stream_second.1.refs_0_ = f32[256,1792]{1,0:T(8,128)S(1)} custom-call(s32[32,28]{1,0:T(8,128)} %refs_0_.11, s32[32,28]{1,0:T(8,128)} %refs_1_.7, bf16[4096,3584]{1,0:T(8,128)(2,1)} %refs_2_.7, bf16[4096,3584]{1,0:T(8,128)(2,1)} %refs_3_.7, bf16[32,4096]{1,0:T(8,128)(2,1)S(1)} %tie.9.refs_0_.refs_4_, bf16[32,4096]{1,0:T(8,128)(2,1)S(1)} %tie.11.refs_1_.refs_5_, ...), custom_call_target="tpu_custom_call" | custom-call | flops 3758096384 | bytes 14680064 | tf_op jit(solution)/shard_map/stream_second/pallas_call | solution.py:234
  40.0 1.6 %collective-permute-start.10 = (bf16[256,1792]{1,0:T(8,128)(2,1)S(1)}, bf16[256,1792]{1,0:T(8,128)(2,1)S(1)}, u32[]{:S(2)}, u32[]{:S(2)}) collective-permute-start(bf16[256,1792]{1,0:T(8,128)(2,1)S(1)} %added.1.refs_5_), channel_id=1, source_target_pairs={{0,16},{1,9},{2,18},{3,11},{4,20},{5,13},{6,22},{7,15},{8,24},{9,1... | collective-permute-start | bytes 2752520 | tf_op jit(solution)/shard_map/ppermute | solution.py:383
  41.6 2.1 %held_pairs.7.refs_12_ = bf16[128,1792]{1,0:T(8,128)(2,1)S(1)} custom-call(bf16[32,4096]{1,0:T(8,128)(2,1)S(1)} %tie.9.refs_0_.refs_4_, bf16[32,4096]{1,0:T(8,128)(2,1)S(1)} %tie.11.refs_1_.refs_5_, bf16[32,4096]{1,0:T(8,128)(2,1)S(1)} %collective-permute-done.5.refs_2_.refs_6_, bf16[32,4096]{1,0:T(8,128)(2,1)S(1)} %collective-permute-done.6.refs_3_.refs_7_, ...), custom_call_target="tpu_custom_call" | custom-call | flops 1879048192 | bytes 7340032 | tf_op jit(solution)/shard_map/held_pairs/pallas_call | solution.py:199
  45.2 6.8 %stream_own.1 = (f32[128,1792]{1,0:T(8,128)S(1)}, f32[128,1792]{1,0:T(8,128)S(1)}) custom-call(s32[32,28]{1,0:T(8,128)} %refs_0_.11, s32[32,28]{1,0:T(8,128)} %refs_1_.7, bf16[4096,3584]{1,0:T(8,128)(2,1)} %refs_2_.7, bf16[4096,3584]{1,0:T(8,128)(2,1)} %refs_3_.7, bf16[32,4096]{1,0:T(8,128)(2,1)S(1)} %tie.9.refs_0_.refs_4_, ...), custom_call_target="tpu_custom_call" | custom-call | flops 3758096384 | bytes 14680064 | tf_op jit(solution)/shard_map/stream_own/pallas_call | solution.py:234
  52.1 5.8 %load_down.2 = (bf16[7,128,4096]{2,1,0:T(8,128)(2,1)S(1)}, bf16[7,128,4096]{2,1,0:T(8,128)(2,1)S(1)}) custom-call(s32[28,32]{1,0:T(8,128)} %mask_hbm.3, bf16[3584,4096]{1,0:T(8,128)(2,1)} %down_hbm.3, f32[128,1792]{1,0:T(8,128)S(1)} %get-tuple-element.16.refs_0_.own), custom_call_target="tpu_custom_call" | custom-call | bytes 14680064 | tf_op jit(solution)/shard_map/load_down/pallas_call | solution.py:278
  58.6 1.6 %collective-permute-start.12 = (bf16[128,896]{1,0:T(8,128)(2,1)S(1)}, bf16[128,896]{1,0:T(8,128)(2,1)S(1)}, u32[]{:S(2)}, u32[]{:S(2)}) collective-permute-start(bf16[128,896]{1,0:T(8,128)(2,1)S(1)} %gated.2.refs_0_), channel_id=1, source_target_pairs={{0,16},{1,9},{2,18},{3,11},{4,20},{5,13},{6,22},{7,15},{8,24},{9,1... | collective-permute-start | bytes 688136 | tf_op jit(solution)/shard_map/ppermute | solution.py:383
  61.9 5.7 %load_down.3 = (bf16[7,128,4096]{2,1,0:T(8,128)(2,1)S(1)}, bf16[7,128,4096]{2,1,0:T(8,128)(2,1)S(1)}) custom-call(s32[28,32]{1,0:T(8,128)} %mask_hbm.3, bf16[3584,4096]{1,0:T(8,128)(2,1)} %down_hbm.3, bf16[128,896]{1,0:T(8,128)(2,1)S(1)} %gated.3.refs_0_), custom_call_target="tpu_custom_call" | custom-call | bytes 14680064 | tf_op jit(solution)/shard_map/load_down/pallas_call | solution.py:278
  68.6 1.6 %collective-permute-start.16 = (bf16[128,896]{1,0:T(8,128)(2,1)S(1)}, bf16[128,896]{1,0:T(8,128)(2,1)S(1)}, u32[]{:S(2)}, u32[]{:S(2)}) collective-permute-start(bf16[128,896]{1,0:T(8,128)(2,1)S(1)} %tie.14.refs_0_), channel_id=1, source_target_pairs={{0,8},{1,17},{2,10},{3,19},{4,12},{5,21},{6,14},{7,23},{8,0},{9,25... | collective-permute-start | bytes 688136 | tf_op jit(solution)/shard_map/ppermute | solution.py:383
  70.2 3.8 %down.5.refs_2_ = f32[128,4096]{1,0:T(8,128)S(1)} custom-call(bf16[128,896]{1,0:T(8,128)(2,1)S(1)} %gated.2.refs_0_, bf16[128,896]{1,0:T(8,128)(2,1)S(1)} %tie.13.refs_1_, bf16[128,896]{1,0:T(8,128)(2,1)S(1)} %collective-permute-done.15.refs_2_, bf16[7,128,4096]{2,1,0:T(8,128)(2,1)S(1)} %get-tuple-element.17.refs_0_.refs_3_.refs_1_, ...), custom_call_target="tpu_custom_call" | custom-call | flops 2818572288 | bytes 22020096 | tf_op jit(solution)/shard_map/down/pallas_call | solution.py:318
  74.0 1.9 %down.6 = (f32[64,4096]{1,0:T(8,128)S(1)}, f32[64,4096]{1,0:T(8,128)S(1)}) custom-call(bf16[128,896]{1,0:T(8,128)(2,1)S(1)} %collective-permute-done.14.refs_0_, bf16[7,128,4096]{2,1,0:T(8,128)(2,1)S(1)} %get-tuple-element.18.refs_1_, f32[128,4096]{1,0:T(8,128)S(1)} %down.5.refs_2_), custom_call_target="tpu_custom_call" | custom-call | flops 939524096 | bytes 7340032 | tf_op jit(solution)/shard_map/down/pallas_call | solution.py:318
  76.1 1.9 %down.7.refs_1_.refs_4_ = f32[128,4096]{1,0:T(8,128)S(1)} custom-call(bf16[128,896]{1,0:T(8,128)(2,1)S(1)} %tie.14.refs_0_, bf16[7,128,4096]{2,1,0:T(8,128)(2,1)S(1)} %get-tuple-element.17.refs_0_.refs_3_.refs_1_, f32[64,4096]{1,0:T(8,128)S(1)} %tie.15.refs_2_), custom_call_target="tpu_custom_call" | custom-call | flops 939524096 | bytes 7340032 | tf_op jit(solution)/shard_map/down/pallas_call | solution.py:318
  80.1 2.8 %down.8.refs_2_ = f32[128,4096]{1,0:T(8,128)S(1)} custom-call(bf16[128,896]{1,0:T(8,128)(2,1)S(1)} %tie.16.refs_0_, bf16[128,896]{1,0:T(8,128)(2,1)S(1)} %collective-permute-done.16.refs_2_.refs_1_, bf16[7,128,4096]{2,1,0:T(8,128)(2,1)S(1)} %get-tuple-element.19.refs_4_.refs_2_, bf16[7,128,4096]{2,1,0:T(8,128)(2,1)S(1)} %get-tuple-element.20.refs_5_.refs_3_, ...), custom_call_target="tpu_custom_call" | custom-call | flops 1879048192 | bytes 14680064 | tf_op jit(solution)/shard_map/down/pallas_call | solution.py:318
  84.1 1.9 %down.9 = (f32[64,4096]{1,0:T(8,128)S(1)}, f32[64,4096]{1,0:T(8,128)S(1)}) custom-call(bf16[128,896]{1,0:T(8,128)(2,1)S(1)} %collective-permute-done.17.refs_0_, bf16[7,128,4096]{2,1,0:T(8,128)(2,1)S(1)} %get-tuple-element.18.refs_1_, f32[128,4096]{1,0:T(8,128)S(1)} %down.8.refs_2_), custom_call_target="tpu_custom_call" | custom-call | flops 939524096 | bytes 7340032 | tf_op jit(solution)/shard_map/down/pallas_call | solution.py:318
  85.9 2.2 %collective-permute-done.19 = bf16[32,4096]{1,0:T(8,128)(2,1)S(1)} collective-permute-done((bf16[32,4096]{1,0:T(8,128)(2,1)S(1)}, bf16[32,4096]{1,0:T(8,128)(2,1)S(1)}, u32[]{:S(2)}, u32[]{:S(2)}) %collective-permute-start.19) | collective-permute-done | bytes 262176 | tf_op jit(solution)/shard_map/ppermute | solution.py:383
  88.4 2.2 %collective-permute-start.22 = (bf16[32,4096]{1,0:T(8,128)(2,1)S(1)}, bf16[32,4096]{1,0:T(8,128)(2,1)S(1)}, u32[]{:S(2)}, u32[]{:S(2)}) collective-permute-start(bf16[32,4096]{1,0:T(8,128)(2,1)S(1)} %fusion.2.refs_1_), channel_id=1, source_target_pairs={{0,4},{1,5},{2,6},{3,7},{4,0},{5,1},{6,2},{7,3},{8,12},{9,13},{10,... | collective-permute-start | bytes 786440 | tf_op jit(solution)/shard_map/ppermute | solution.py:383
  92.3 11.3 %collective-permute-done.22 = bf16[32,4096]{1,0:T(8,128)(2,1)S(1)} collective-permute-done((bf16[32,4096]{1,0:T(8,128)(2,1)S(1)}, bf16[32,4096]{1,0:T(8,128)(2,1)S(1)}, u32[]{:S(2)}, u32[]{:S(2)}) %collective-permute-start.22) | collective-permute-done | bytes 262176 | tf_op jit(solution)/shard_map/ppermute | solution.py:383
  (57 shorter events, 19.7 us)
Async XLA Ops:
  0.0 17.6 %collective-permute-start.2 = (bf16[32,4096]{1,0:T(8,128)(2,1)}, bf16[32,4096]{1,0:T(8,128)(2,1)S(1)}, u32[]{:S(2)}, u32[]{:S(2)}) collective-permute-start(bf16[32,4096]{1,0:T(8,128)(2,1)} %refs_8_.3), channel_id=1, source_target_pairs={{0,2},{1,3},{2,0},{3,1},{4,6},{5,7},{6,4},{7,5},{8,10},{9,11},{10,... | collective-permute-start | bytes 786440 | tf_op jit(solution)/shard_map/ppermute | solution.py:383
  3.0 15.5 %collective-permute-start.3 = (bf16[32,4096]{1,0:T(8,128)(2,1)}, bf16[32,4096]{1,0:T(8,128)(2,1)S(1)}, u32[]{:S(2)}, u32[]{:S(2)}) collective-permute-start(bf16[32,4096]{1,0:T(8,128)(2,1)} %refs_8_.3), channel_id=1, source_target_pairs={{0,1},{1,0},{2,3},{3,2},{4,5},{5,4},{6,7},{7,6},{8,9},{9,8},{10,11... | collective-permute-start | bytes 786440 | tf_op jit(solution)/shard_map/ppermute | solution.py:383
  3.0 15.5 %collective-permute-start = (bf16[32,4096]{1,0:T(8,128)(2,1)}, bf16[32,4096]{1,0:T(8,128)(2,1)S(1)}, u32[]{:S(2)}, u32[]{:S(2)}) collective-permute-start(bf16[32,4096]{1,0:T(8,128)(2,1)} %refs_8_.3), channel_id=1, source_target_pairs={{0,4},{1,5},{2,6},{3,7},{4,0},{5,1},{6,2},{7,3},{8,12},{9,13},{10,... | collective-permute-start | bytes 786440 | tf_op jit(solution)/shard_map/ppermute | solution.py:383
  17.6 1.6 %copy-start = (bf16[32,4096]{1,0:T(8,128)(2,1)S(1)}, bf16[32,4096]{1,0:T(8,128)(2,1)}, u32[]{:S(2)}) copy-start(bf16[32,4096]{1,0:T(8,128)(2,1)} %refs_8_.3) | copy-start | bytes 786436
  17.6 1.6 %collective-permute-start.4 = (bf16[32,4096]{1,0:T(8,128)(2,1)S(1)}, bf16[32,4096]{1,0:T(8,128)(2,1)S(1)}, u32[]{:S(2)}, u32[]{:S(2)}) collective-permute-start(bf16[32,4096]{1,0:T(8,128)(2,1)S(1)} %tie.10.refs_1_.refs_9_), channel_id=1, source_target_pairs={{0,1},{1,0},{2,3},{3,2},{4,5},{5,4},{6,7},{7,6},{8,9},{9,8},{10,11... | collective-permute-start | bytes 786440 | tf_op jit(solution)/shard_map/ppermute | solution.py:383
  18.5 7.9 %collective-permute-start.1 = (bf16[32,4096]{1,0:T(8,128)(2,1)S(1)}, bf16[32,4096]{1,0:T(8,128)(2,1)S(1)}, u32[]{:S(2)}, u32[]{:S(2)}) collective-permute-start(bf16[32,4096]{1,0:T(8,128)(2,1)S(1)} %tie.9.refs_0_.refs_4_), channel_id=1, source_target_pairs={{0,2},{1,3},{2,0},{3,1},{4,6},{5,7},{6,4},{7,5},{8,10},{9,11},{10,... | collective-permute-start | bytes 786440 | tf_op jit(solution)/shard_map/ppermute | solution.py:383
  18.5 9.4 %collective-permute-start.5 = (bf16[32,4096]{1,0:T(8,128)(2,1)S(1)}, bf16[32,4096]{1,0:T(8,128)(2,1)S(1)}, u32[]{:S(2)}, u32[]{:S(2)}) collective-permute-start(bf16[32,4096]{1,0:T(8,128)(2,1)S(1)} %tie.9.refs_0_.refs_4_), channel_id=1, source_target_pairs={{0,1},{1,0},{2,3},{3,2},{4,5},{5,4},{6,7},{7,6},{8,9},{9,8},{10,11... | collective-permute-start | bytes 786440 | tf_op jit(solution)/shard_map/ppermute | solution.py:383
  21.3 8.8 %collective-permute-start.7 = (bf16[128,1792]{1,0:T(8,128)(2,1)S(1)}, bf16[128,1792]{1,0:T(8,128)(2,1)S(1)}, u32[]{:S(2)}, u32[]{:S(2)}) collective-permute-start(bf16[128,1792]{1,0:T(8,128)(2,1)S(1)} %held_pairs.4.refs_5_), channel_id=1, source_target_pairs={{0,8},{1,17},{2,10},{3,19},{4,12},{5,21},{6,14},{7,23},{8,0},{9,25... | collective-permute-start | bytes 1376264 | tf_op jit(solution)/shard_map/ppermute | solution.py:383
  26.5 1.5 %collective-permute-start.6 = (bf16[32,4096]{1,0:T(8,128)(2,1)S(1)}, bf16[32,4096]{1,0:T(8,128)(2,1)S(1)}, u32[]{:S(2)}, u32[]{:S(2)}) collective-permute-start(bf16[32,4096]{1,0:T(8,128)(2,1)S(1)} %tie.11.refs_1_.refs_5_), channel_id=1, source_target_pairs={{0,1},{1,0},{2,3},{3,2},{4,5},{5,4},{6,7},{7,6},{8,9},{9,8},{10,11... | collective-permute-start | bytes 786440 | tf_op jit(solution)/shard_map/ppermute | solution.py:383
  26.5 12.1 %collective-permute-start.9 = (bf16[128,1792]{1,0:T(8,128)(2,1)S(1)}, bf16[128,1792]{1,0:T(8,128)(2,1)S(1)}, u32[]{:S(2)}, u32[]{:S(2)}) collective-permute-start(bf16[128,1792]{1,0:T(8,128)(2,1)S(1)} %held_pairs.5.refs_1_.refs_13_), channel_id=1, source_target_pairs={{0,8},{1,17},{2,10},{3,19},{4,12},{5,21},{6,14},{7,23},{8,0},{9,25... | collective-permute-start | bytes 1376264 | tf_op jit(solution)/shard_map/ppermute | solution.py:383
  30.1 9.8 %collective-permute-start.8 = (bf16[128,1792]{1,0:T(8,128)(2,1)S(1)}, bf16[128,1792]{1,0:T(8,128)(2,1)S(1)}, u32[]{:S(2)}, u32[]{:S(2)}) collective-permute-start(bf16[128,1792]{1,0:T(8,128)(2,1)S(1)} %tie.12.refs_12_), channel_id=1, source_target_pairs={{0,8},{1,17},{2,10},{3,19},{4,12},{5,21},{6,14},{7,23},{8,0},{9,25... | collective-permute-start | bytes 1376264 | tf_op jit(solution)/shard_map/ppermute | solution.py:383
  40.0 18.4 %collective-permute-start.10 = (bf16[256,1792]{1,0:T(8,128)(2,1)S(1)}, bf16[256,1792]{1,0:T(8,128)(2,1)S(1)}, u32[]{:S(2)}, u32[]{:S(2)}) collective-permute-start(bf16[256,1792]{1,0:T(8,128)(2,1)S(1)} %added.1.refs_5_), channel_id=1, source_target_pairs={{0,16},{1,9},{2,18},{3,11},{4,20},{5,13},{6,22},{7,15},{8,24},{9,1... | collective-permute-start | bytes 2752520 | tf_op jit(solution)/shard_map/ppermute | solution.py:383
  43.7 14.2 %collective-permute-start.11 = (bf16[128,1792]{1,0:T(8,128)(2,1)S(1)}, bf16[128,1792]{1,0:T(8,128)(2,1)S(1)}, u32[]{:S(2)}, u32[]{:S(2)}) collective-permute-start(bf16[128,1792]{1,0:T(8,128)(2,1)S(1)} %held_pairs.7.refs_12_), channel_id=1, source_target_pairs={{0,8},{1,17},{2,10},{3,19},{4,12},{5,21},{6,14},{7,23},{8,0},{9,25... | collective-permute-start | bytes 1376264 | tf_op jit(solution)/shard_map/ppermute | solution.py:383
  58.6 9.0 %collective-permute-start.12 = (bf16[128,896]{1,0:T(8,128)(2,1)S(1)}, bf16[128,896]{1,0:T(8,128)(2,1)S(1)}, u32[]{:S(2)}, u32[]{:S(2)}) collective-permute-start(bf16[128,896]{1,0:T(8,128)(2,1)S(1)} %gated.2.refs_0_), channel_id=1, source_target_pairs={{0,16},{1,9},{2,18},{3,11},{4,20},{5,13},{6,22},{7,15},{8,24},{9,1... | collective-permute-start | bytes 688136 | tf_op jit(solution)/shard_map/ppermute | solution.py:383
  60.2 10.1 %collective-permute-start.15 = (bf16[128,896]{1,0:T(8,128)(2,1)S(1)}, bf16[128,896]{1,0:T(8,128)(2,1)S(1)}, u32[]{:S(2)}, u32[]{:S(2)}) collective-permute-start(bf16[128,896]{1,0:T(8,128)(2,1)S(1)} %gated.2.refs_0_), channel_id=1, source_target_pairs={{0,8},{1,17},{2,10},{3,19},{4,12},{5,21},{6,14},{7,23},{8,0},{9,25... | collective-permute-start | bytes 688136 | tf_op jit(solution)/shard_map/ppermute | solution.py:383
  67.6 6.5 %collective-permute-start.14 = (bf16[128,896]{1,0:T(8,128)(2,1)S(1)}, bf16[128,896]{1,0:T(8,128)(2,1)S(1)}, u32[]{:S(2)}, u32[]{:S(2)}) collective-permute-start(bf16[128,896]{1,0:T(8,128)(2,1)S(1)} %tie.13.refs_1_), channel_id=1, source_target_pairs={{0,8},{1,17},{2,10},{3,19},{4,12},{5,21},{6,14},{7,23},{8,0},{9,25... | collective-permute-start | bytes 688136 | tf_op jit(solution)/shard_map/ppermute | solution.py:383
  68.1 7.8 %collective-permute-start.13 = (bf16[128,896]{1,0:T(8,128)(2,1)S(1)}, bf16[128,896]{1,0:T(8,128)(2,1)S(1)}, u32[]{:S(2)}, u32[]{:S(2)}) collective-permute-start(bf16[128,896]{1,0:T(8,128)(2,1)S(1)} %tie.14.refs_0_), channel_id=1, source_target_pairs={{0,16},{1,9},{2,18},{3,11},{4,20},{5,13},{6,22},{7,15},{8,24},{9,1... | collective-permute-start | bytes 688136 | tf_op jit(solution)/shard_map/ppermute | solution.py:383
  68.6 7.5 %collective-permute-start.16 = (bf16[128,896]{1,0:T(8,128)(2,1)S(1)}, bf16[128,896]{1,0:T(8,128)(2,1)S(1)}, u32[]{:S(2)}, u32[]{:S(2)}) collective-permute-start(bf16[128,896]{1,0:T(8,128)(2,1)S(1)} %tie.14.refs_0_), channel_id=1, source_target_pairs={{0,8},{1,17},{2,10},{3,19},{4,12},{5,21},{6,14},{7,23},{8,0},{9,25... | collective-permute-start | bytes 688136 | tf_op jit(solution)/shard_map/ppermute | solution.py:383
  76.1 2.7 %collective-permute-start.18 = (f32[64,4096]{1,0:T(8,128)S(1)}, f32[64,4096]{1,0:T(8,128)S(1)}, u32[]{:S(2)}, u32[]{:S(2)}) collective-permute-start(f32[64,4096]{1,0:T(8,128)S(1)} %tie.15.refs_2_), channel_id=1, source_target_pairs={{0,1},{1,0},{2,3},{3,2},{4,5},{5,4},{6,7},{7,6},{8,9},{9,8},{10,11... | collective-permute-start | bytes 3145736 | tf_op jit(solution)/shard_map/ppermute | solution.py:383
  78.0 6.1 %collective-permute-start.17 = (bf16[128,896]{1,0:T(8,128)(2,1)S(1)}, bf16[128,896]{1,0:T(8,128)(2,1)S(1)}, u32[]{:S(2)}, u32[]{:S(2)}) collective-permute-start(bf16[128,896]{1,0:T(8,128)(2,1)S(1)} %tie.16.refs_0_), channel_id=1, source_target_pairs={{0,8},{1,17},{2,10},{3,19},{4,12},{5,21},{6,14},{7,23},{8,0},{9,25... | collective-permute-start | bytes 688136 | tf_op jit(solution)/shard_map/ppermute | solution.py:383
  78.9 9.2 %collective-permute-start.19 = (bf16[32,4096]{1,0:T(8,128)(2,1)S(1)}, bf16[32,4096]{1,0:T(8,128)(2,1)S(1)}, u32[]{:S(2)}, u32[]{:S(2)}) collective-permute-start(bf16[32,4096]{1,0:T(8,128)(2,1)S(1)} %slice.33.refs_5_), channel_id=1, source_target_pairs={{0,2},{1,3},{2,0},{3,1},{4,6},{5,7},{6,4},{7,5},{8,10},{9,11},{10,... | collective-permute-start | bytes 786440 | tf_op jit(solution)/shard_map/ppermute | solution.py:383
  88.2 2.7 %collective-permute-start.20 = (f32[64,4096]{1,0:T(8,128)S(1)}, f32[64,4096]{1,0:T(8,128)S(1)}, u32[]{:S(2)}, u32[]{:S(2)}) collective-permute-start(f32[64,4096]{1,0:T(8,128)S(1)} %tie.17), channel_id=1, source_target_pairs={{0,1},{1,0},{2,3},{3,2},{4,5},{5,4},{6,7},{7,6},{8,9},{9,8},{10,11... | collective-permute-start | bytes 3145736 | tf_op jit(solution)/shard_map/ppermute | solution.py:383
  88.4 15.3 %collective-permute-start.22 = (bf16[32,4096]{1,0:T(8,128)(2,1)S(1)}, bf16[32,4096]{1,0:T(8,128)(2,1)S(1)}, u32[]{:S(2)}, u32[]{:S(2)}) collective-permute-start(bf16[32,4096]{1,0:T(8,128)(2,1)S(1)} %fusion.2.refs_1_), channel_id=1, source_target_pairs={{0,4},{1,5},{2,6},{3,7},{4,0},{5,1},{6,2},{7,3},{8,12},{9,13},{10,... | collective-permute-start | bytes 786440 | tf_op jit(solution)/shard_map/ppermute | solution.py:383
  91.1 13.3 %collective-permute-start.21 = (bf16[32,4096]{1,0:T(8,128)(2,1)S(1)}, bf16[32,4096]{1,0:T(8,128)(2,1)S(1)}, u32[]{:S(2)}, u32[]{:S(2)}) collective-permute-start(bf16[32,4096]{1,0:T(8,128)(2,1)S(1)} %slice.32), channel_id=1, source_target_pairs={{0,2},{1,3},{2,0},{3,1},{4,6},{5,7},{6,4},{7,5},{8,10},{9,11},{10,... | collective-permute-start | bytes 786440 | tf_op jit(solution)/shard_map/ppermute | solution.py:383

commit v3 on v2

--- a/solution.py
+++ b/solution.py
@@ -309,7 +309,7 @@
         for k, out in enumerate(outs):
             out[:, at] = value[k * size : (k + 1) * size]
 
-    loop(width // tile, step, unroll=2)
+    loop(width // tile, step, unroll=width // tile)
 
 
 def down(hidden, bufs, total=(), blocks=1, tile=512, deps=()):

time: 106 us -> 105 us (level)
  Pallas kernels: 58.1 us -> 55 us
  waiting for transfers between devices: 20.9 us -> 23.5 us
    pallas_call x5, Pallas kernels: 12.1 us -> 9.04 us  [down(): pl.pallas_call(functools.partial(down_kernel, count, len(total), blocks,...]
    ppermute x23, waiting for transfers between devices: 20.9 us -> 23.5 us  [swap(): return lax.ppermute(value, ('row', 'col'), pairs)]
  transfers between devices with their start and end apart: 23 -> 23, of which waited for: 12 -> 14; matrix products, arithmetic and copies ran while one was open for 0% -> 0% of each run, Pallas kernels for 55% -> 52%
where the time goes in v3:
time: 105 us
  Pallas kernels  55 us (52%)
  starting transfers between devices  24.8 us (24%)
  waiting for transfers between devices  23.5 us (22%)
  other arithmetic  1.05 us (1%)
    ppermute x23, starting transfers between devices, swap(): return lax.ppermute(value, ('row', 'col'), pairs)  24.8 us
    ppermute x23, waiting for transfers between devices, swap(): return lax.ppermute(value, ('row', 'col'), pairs)  23.5 us
    pallas_call x2, Pallas kernels, stream_pairs(): pl.pallas_call(functools.partial(stream_pairs_kernel, name, len(x), rows)...  13.7 us
    pallas_call x2, Pallas kernels, load_pairs(): pl.pallas_call(functools.partial(load_pairs_kernel, name), in_specs=[HBM_...  12 us
    pallas_call x2, Pallas kernels, load_down(): pl.pallas_call(functools.partial(load_down_kernel, names), in_specs=[HBM_...  11.5 us
    pallas_call x5, Pallas kernels, down(): pl.pallas_call(functools.partial(down_kernel, count, len(total), blocks,...  9.04 us
    pallas_call x4, Pallas kernels, held_pairs(): pl.pallas_call(functools.partial(held_pairs_kernel, len(x)), in_specs=[VM...  8.25 us
  transfers between devices with their start and end apart: 23, of which 14 were waited for; matrix products, arithmetic and copies ran while one was open for 0% of the time, Pallas kernels for 52%

profile of v3, /device:TPU:0, one launch (start us, length us, event | category | flops | bytes accessed | tf_op | source)
XLA Modules:
  0.0 104.6 jit_solution(17383564198357214320)
XLA Ops:
  0.0 3.0 %collective-permute-start.2 = (bf16[32,4096]{1,0:T(8,128)(2,1)}, bf16[32,4096]{1,0:T(8,128)(2,1)S(1)}, u32[]{:S(2)}, u32[]{:S(2)}) collective-permute-start(bf16[32,4096]{1,0:T(8,128)(2,1)} %refs_8_.3), channel_id=1, source_target_pairs={{0,2},{1,3},{2,0},{3,1},{4,6},{5,7},{6,4},{7,5},{8,10},{9,11},{10,... | collective-permute-start | bytes 786440 | tf_op jit(solution)/shard_map/ppermute | solution.py:383
  3.0 2.6 %collective-permute-start = (bf16[32,4096]{1,0:T(8,128)(2,1)}, bf16[32,4096]{1,0:T(8,128)(2,1)S(1)}, u32[]{:S(2)}, u32[]{:S(2)}) collective-permute-start(bf16[32,4096]{1,0:T(8,128)(2,1)} %refs_8_.3), channel_id=1, source_target_pairs={{0,4},{1,5},{2,6},{3,7},{4,0},{5,1},{6,2},{7,3},{8,12},{9,13},{10,... | collective-permute-start | bytes 786440 | tf_op jit(solution)/shard_map/ppermute | solution.py:383
  5.6 6.0 %load_last.1.refs_4_ = bf16[7,4096,256]{2,1,0:T(8,128)(2,1)S(1)} custom-call(s32[32,28]{1,0:T(8,128)} %refs_0_.11, s32[32,28]{1,0:T(8,128)} %refs_1_.7, bf16[4096,3584]{1,0:T(8,128)(2,1)} %refs_2_.7, bf16[4096,3584]{1,0:T(8,128)(2,1)} %refs_3_.7), custom_call_target="tpu_custom_call" | custom-call | bytes 14680064 | tf_op jit(solution)/shard_map/load_last/pallas_call | solution.py:174
  11.6 6.0 %load_first.1.refs_1_.refs_4_ = bf16[7,4096,256]{2,1,0:T(8,128)(2,1)S(1)} custom-call(s32[32,28]{1,0:T(8,128)} %refs_0_.11, s32[32,28]{1,0:T(8,128)} %refs_1_.7, bf16[4096,3584]{1,0:T(8,128)(2,1)} %refs_2_.7, bf16[4096,3584]{1,0:T(8,128)(2,1)} %refs_3_.7, bf16[7,4096,256]{2,1,0:T(8,128)(2,1)S(1)} %load_last.1.refs_4_), custom_call_target="tpu_custom_call" | custom-call | bytes 14680064 | tf_op jit(solution)/shard_map/load_first/pallas_call | solution.py:174
  19.2 2.1 %held_pairs.4.refs_5_ = bf16[128,1792]{1,0:T(8,128)(2,1)S(1)} custom-call(bf16[32,4096]{1,0:T(8,128)(2,1)S(1)} %copy-done, bf16[32,4096]{1,0:T(8,128)(2,1)S(1)} %tie.10.refs_1_.refs_9_, bf16[32,4096]{1,0:T(8,128)(2,1)S(1)} %collective-permute-done.3.refs_2_.refs_10_, bf16[32,4096]{1,0:T(8,128)(2,1)S(1)} %collective-permute-done.4.refs_3_.refs_11_, ...), custom_call_target="tpu_custom_call" | custom-call | flops 1879048192 | bytes 7340032 | tf_op jit(solution)/shard_map/held_pairs/pallas_call | solution.py:199
  21.3 1.6 %collective-permute-start.7 = (bf16[128,1792]{1,0:T(8,128)(2,1)S(1)}, bf16[128,1792]{1,0:T(8,128)(2,1)S(1)}, u32[]{:S(2)}, u32[]{:S(2)}) collective-permute-start(bf16[128,1792]{1,0:T(8,128)(2,1)S(1)} %held_pairs.4.refs_5_), channel_id=1, source_target_pairs={{0,8},{1,17},{2,10},{3,19},{4,12},{5,21},{6,14},{7,23},{8,0},{9,25... | collective-permute-start | bytes 1376264 | tf_op jit(solution)/shard_map/ppermute | solution.py:383
  22.9 2.1 %held_pairs.5.refs_1_.refs_13_ = bf16[128,1792]{1,0:T(8,128)(2,1)S(1)} custom-call(bf16[32,4096]{1,0:T(8,128)(2,1)S(1)} %copy-done, bf16[32,4096]{1,0:T(8,128)(2,1)S(1)} %tie.10.refs_1_.refs_9_, bf16[32,4096]{1,0:T(8,128)(2,1)S(1)} %collective-permute-done.3.refs_2_.refs_10_, bf16[32,4096]{1,0:T(8,128)(2,1)S(1)} %collective-permute-done.4.refs_3_.refs_11_, ...), custom_call_target="tpu_custom_call" | custom-call | flops 1879048192 | bytes 7340032 | tf_op jit(solution)/shard_map/held_pairs/pallas_call | solution.py:199
  24.9 1.5 %collective-permute-done.1.refs_0_ = bf16[32,4096]{1,0:T(8,128)(2,1)S(1)} collective-permute-done((bf16[32,4096]{1,0:T(8,128)(2,1)S(1)}, bf16[32,4096]{1,0:T(8,128)(2,1)S(1)}, u32[]{:S(2)}, u32[]{:S(2)}) %collective-permute-start.1) | collective-permute-done | bytes 262176 | tf_op jit(solution)/shard_map/ppermute | solution.py:383
  28.0 2.1 %held_pairs.6.refs_0_ = bf16[128,1792]{1,0:T(8,128)(2,1)S(1)} custom-call(bf16[32,4096]{1,0:T(8,128)(2,1)S(1)} %tie.9.refs_0_.refs_4_, bf16[32,4096]{1,0:T(8,128)(2,1)S(1)} %tie.11.refs_1_.refs_5_, bf16[32,4096]{1,0:T(8,128)(2,1)S(1)} %collective-permute-done.5.refs_2_.refs_6_, bf16[32,4096]{1,0:T(8,128)(2,1)S(1)} %collective-permute-done.6.refs_3_.refs_7_, ...), custom_call_target="tpu_custom_call" | custom-call | flops 1879048192 | bytes 7340032 | tf_op jit(solution)/shard_map/held_pairs/pallas_call | solution.py:199
  30.1 1.6 %collective-permute-start.8 = (bf16[128,1792]{1,0:T(8,128)(2,1)S(1)}, bf16[128,1792]{1,0:T(8,128)(2,1)S(1)}, u32[]{:S(2)}, u32[]{:S(2)}) collective-permute-start(bf16[128,1792]{1,0:T(8,128)(2,1)S(1)} %tie.12.refs_12_), channel_id=1, source_target_pairs={{0,8},{1,17},{2,10},{3,19},{4,12},{5,21},{6,14},{7,23},{8,0},{9,25... | collective-permute-start | bytes 1376264 | tf_op jit(solution)/shard_map/ppermute | solution.py:383
  31.6 6.9 %stream_second.1.refs_0_ = f32[256,1792]{1,0:T(8,128)S(1)} custom-call(s32[32,28]{1,0:T(8,128)} %refs_0_.11, s32[32,28]{1,0:T(8,128)} %refs_1_.7, bf16[4096,3584]{1,0:T(8,128)(2,1)} %refs_2_.7, bf16[4096,3584]{1,0:T(8,128)(2,1)} %refs_3_.7, bf16[32,4096]{1,0:T(8,128)(2,1)S(1)} %tie.9.refs_0_.refs_4_, bf16[32,4096]{1,0:T(8,128)(2,1)S(1)} %tie.11.refs_1_.refs_5_, ...), custom_call_target="tpu_custom_call" | custom-call | flops 3758096384 | bytes 14680064 | tf_op jit(solution)/shard_map/stream_second/pallas_call | solution.py:234
  40.0 1.6 %collective-permute-start.10 = (bf16[256,1792]{1,0:T(8,128)(2,1)S(1)}, bf16[256,1792]{1,0:T(8,128)(2,1)S(1)}, u32[]{:S(2)}, u32[]{:S(2)}) collective-permute-start(bf16[256,1792]{1,0:T(8,128)(2,1)S(1)} %added.1.refs_5_), channel_id=1, source_target_pairs={{0,16},{1,9},{2,18},{3,11},{4,20},{5,13},{6,22},{7,15},{8,24},{9,1... | collective-permute-start | bytes 2752520 | tf_op jit(solution)/shard_map/ppermute | solution.py:383
  41.6 2.1 %held_pairs.7.refs_12_ = bf16[128,1792]{1,0:T(8,128)(2,1)S(1)} custom-call(bf16[32,4096]{1,0:T(8,128)(2,1)S(1)} %tie.9.refs_0_.refs_4_, bf16[32,4096]{1,0:T(8,128)(2,1)S(1)} %tie.11.refs_1_.refs_5_, bf16[32,4096]{1,0:T(8,128)(2,1)S(1)} %collective-permute-done.5.refs_2_.refs_6_, bf16[32,4096]{1,0:T(8,128)(2,1)S(1)} %collective-permute-done.6.refs_3_.refs_7_, ...), custom_call_target="tpu_custom_call" | custom-call | flops 1879048192 | bytes 7340032 | tf_op jit(solution)/shard_map/held_pairs/pallas_call | solution.py:199
  43.7 1.6 %collective-permute-start.11 = (bf16[128,1792]{1,0:T(8,128)(2,1)S(1)}, bf16[128,1792]{1,0:T(8,128)(2,1)S(1)}, u32[]{:S(2)}, u32[]{:S(2)}) collective-permute-start(bf16[128,1792]{1,0:T(8,128)(2,1)S(1)} %held_pairs.7.refs_12_), channel_id=1, source_target_pairs={{0,8},{1,17},{2,10},{3,19},{4,12},{5,21},{6,14},{7,23},{8,0},{9,25... | collective-permute-start | bytes 1376264 | tf_op jit(solution)/shard_map/ppermute | solution.py:383
  45.2 6.8 %stream_own.1 = (f32[128,1792]{1,0:T(8,128)S(1)}, f32[128,1792]{1,0:T(8,128)S(1)}) custom-call(s32[32,28]{1,0:T(8,128)} %refs_0_.11, s32[32,28]{1,0:T(8,128)} %refs_1_.7, bf16[4096,3584]{1,0:T(8,128)(2,1)} %refs_2_.7, bf16[4096,3584]{1,0:T(8,128)(2,1)} %refs_3_.7, bf16[32,4096]{1,0:T(8,128)(2,1)S(1)} %tie.9.refs_0_.refs_4_, ...), custom_call_target="tpu_custom_call" | custom-call | flops 3758096384 | bytes 14680064 | tf_op jit(solution)/shard_map/stream_own/pallas_call | solution.py:234
  52.1 5.8 %load_down.2 = (bf16[7,128,4096]{2,1,0:T(8,128)(2,1)S(1)}, bf16[7,128,4096]{2,1,0:T(8,128)(2,1)S(1)}) custom-call(s32[28,32]{1,0:T(8,128)} %mask_hbm.3, bf16[3584,4096]{1,0:T(8,128)(2,1)} %down_hbm.3, f32[128,1792]{1,0:T(8,128)S(1)} %get-tuple-element.16.refs_0_.own), custom_call_target="tpu_custom_call" | custom-call | bytes 14680064 | tf_op jit(solution)/shard_map/load_down/pallas_call | solution.py:278
  58.6 1.6 %collective-permute-start.12 = (bf16[128,896]{1,0:T(8,128)(2,1)S(1)}, bf16[128,896]{1,0:T(8,128)(2,1)S(1)}, u32[]{:S(2)}, u32[]{:S(2)}) collective-permute-start(bf16[128,896]{1,0:T(8,128)(2,1)S(1)} %gated.2.refs_0_), channel_id=1, source_target_pairs={{0,16},{1,9},{2,18},{3,11},{4,20},{5,13},{6,22},{7,15},{8,24},{9,1... | collective-permute-start | bytes 688136 | tf_op jit(solution)/shard_map/ppermute | solution.py:383
  61.9 5.7 %load_down.3 = (bf16[7,128,4096]{2,1,0:T(8,128)(2,1)S(1)}, bf16[7,128,4096]{2,1,0:T(8,128)(2,1)S(1)}) custom-call(s32[28,32]{1,0:T(8,128)} %mask_hbm.3, bf16[3584,4096]{1,0:T(8,128)(2,1)} %down_hbm.3, bf16[128,896]{1,0:T(8,128)(2,1)S(1)} %gated.3.refs_0_), custom_call_target="tpu_custom_call" | custom-call | bytes 14680064 | tf_op jit(solution)/shard_map/load_down/pallas_call | solution.py:278
  68.6 1.6 %collective-permute-start.16 = (bf16[128,896]{1,0:T(8,128)(2,1)S(1)}, bf16[128,896]{1,0:T(8,128)(2,1)S(1)}, u32[]{:S(2)}, u32[]{:S(2)}) collective-permute-start(bf16[128,896]{1,0:T(8,128)(2,1)S(1)} %tie.14.refs_0_), channel_id=1, source_target_pairs={{0,8},{1,17},{2,10},{3,19},{4,12},{5,21},{6,14},{7,23},{8,0},{9,25... | collective-permute-start | bytes 688136 | tf_op jit(solution)/shard_map/ppermute | solution.py:383
  70.2 3.2 %down.5.refs_2_ = f32[128,4096]{1,0:T(8,128)S(1)} custom-call(bf16[128,896]{1,0:T(8,128)(2,1)S(1)} %gated.2.refs_0_, bf16[128,896]{1,0:T(8,128)(2,1)S(1)} %tie.13.refs_1_, bf16[128,896]{1,0:T(8,128)(2,1)S(1)} %collective-permute-done.15.refs_2_, bf16[7,128,4096]{2,1,0:T(8,128)(2,1)S(1)} %get-tuple-element.17.refs_0_.refs_3_.refs_1_, ...), custom_call_target="tpu_custom_call" | custom-call | flops 2818572288 | bytes 22020096 | tf_op jit(solution)/shard_map/down/pallas_call | solution.py:318
  80.2 2.1 %down.8.refs_2_ = f32[128,4096]{1,0:T(8,128)S(1)} custom-call(bf16[128,896]{1,0:T(8,128)(2,1)S(1)} %tie.16.refs_0_, bf16[128,896]{1,0:T(8,128)(2,1)S(1)} %collective-permute-done.16.refs_2_.refs_1_, bf16[7,128,4096]{2,1,0:T(8,128)(2,1)S(1)} %get-tuple-element.19.refs_4_.refs_2_, bf16[7,128,4096]{2,1,0:T(8,128)(2,1)S(1)} %get-tuple-element.20.refs_5_.refs_3_, ...), custom_call_target="tpu_custom_call" | custom-call | flops 1879048192 | bytes 14680064 | tf_op jit(solution)/shard_map/down/pallas_call | solution.py:318
  84.8 2.8 %collective-permute-done.19 = bf16[32,4096]{1,0:T(8,128)(2,1)S(1)} collective-permute-done((bf16[32,4096]{1,0:T(8,128)(2,1)S(1)}, bf16[32,4096]{1,0:T(8,128)(2,1)S(1)}, u32[]{:S(2)}, u32[]{:S(2)}) %collective-permute-start.19) | collective-permute-done | bytes 262176 | tf_op jit(solution)/shard_map/ppermute | solution.py:383
  87.7 2.2 %collective-permute-start.22 = (bf16[32,4096]{1,0:T(8,128)(2,1)S(1)}, bf16[32,4096]{1,0:T(8,128)(2,1)S(1)}, u32[]{:S(2)}, u32[]{:S(2)}) collective-permute-start(bf16[32,4096]{1,0:T(8,128)(2,1)S(1)} %fusion.2.refs_1_), channel_id=1, source_target_pairs={{0,4},{1,5},{2,6},{3,7},{4,0},{5,1},{6,2},{7,3},{8,12},{9,13},{10,... | collective-permute-start | bytes 786440 | tf_op jit(solution)/shard_map/ppermute | solution.py:383
  91.7 11.3 %collective-permute-done.22 = bf16[32,4096]{1,0:T(8,128)(2,1)S(1)} collective-permute-done((bf16[32,4096]{1,0:T(8,128)(2,1)S(1)}, bf16[32,4096]{1,0:T(8,128)(2,1)S(1)}, u32[]{:S(2)}, u32[]{:S(2)}) %collective-permute-start.22) | collective-permute-done | bytes 262176 | tf_op jit(solution)/shard_map/ppermute | solution.py:383
  (57 shorter events, 20.7 us)
Async XLA Ops:
  0.0 17.6 %collective-permute-start.2 = (bf16[32,4096]{1,0:T(8,128)(2,1)}, bf16[32,4096]{1,0:T(8,128)(2,1)S(1)}, u32[]{:S(2)}, u32[]{:S(2)}) collective-permute-start(bf16[32,4096]{1,0:T(8,128)(2,1)} %refs_8_.3), channel_id=1, source_target_pairs={{0,2},{1,3},{2,0},{3,1},{4,6},{5,7},{6,4},{7,5},{8,10},{9,11},{10,... | collective-permute-start | bytes 786440 | tf_op jit(solution)/shard_map/ppermute | solution.py:383
  3.0 15.5 %collective-permute-start.3 = (bf16[32,4096]{1,0:T(8,128)(2,1)}, bf16[32,4096]{1,0:T(8,128)(2,1)S(1)}, u32[]{:S(2)}, u32[]{:S(2)}) collective-permute-start(bf16[32,4096]{1,0:T(8,128)(2,1)} %refs_8_.3), channel_id=1, source_target_pairs={{0,1},{1,0},{2,3},{3,2},{4,5},{5,4},{6,7},{7,6},{8,9},{9,8},{10,11... | collective-permute-start | bytes 786440 | tf_op jit(solution)/shard_map/ppermute | solution.py:383
  3.0 15.5 %collective-permute-start = (bf16[32,4096]{1,0:T(8,128)(2,1)}, bf16[32,4096]{1,0:T(8,128)(2,1)S(1)}, u32[]{:S(2)}, u32[]{:S(2)}) collective-permute-start(bf16[32,4096]{1,0:T(8,128)(2,1)} %refs_8_.3), channel_id=1, source_target_pairs={{0,4},{1,5},{2,6},{3,7},{4,0},{5,1},{6,2},{7,3},{8,12},{9,13},{10,... | collective-permute-start | bytes 786440 | tf_op jit(solution)/shard_map/ppermute | solution.py:383
  17.6 1.6 %copy-start = (bf16[32,4096]{1,0:T(8,128)(2,1)S(1)}, bf16[32,4096]{1,0:T(8,128)(2,1)}, u32[]{:S(2)}) copy-start(bf16[32,4096]{1,0:T(8,128)(2,1)} %refs_8_.3) | copy-start | bytes 786436
  17.6 1.6 %collective-permute-start.4 = (bf16[32,4096]{1,0:T(8,128)(2,1)S(1)}, bf16[32,4096]{1,0:T(8,128)(2,1)S(1)}, u32[]{:S(2)}, u32[]{:S(2)}) collective-permute-start(bf16[32,4096]{1,0:T(8,128)(2,1)S(1)} %tie.10.refs_1_.refs_9_), channel_id=1, source_target_pairs={{0,1},{1,0},{2,3},{3,2},{4,5},{5,4},{6,7},{7,6},{8,9},{9,8},{10,11... | collective-permute-start | bytes 786440 | tf_op jit(solution)/shard_map/ppermute | solution.py:383
  18.5 7.9 %collective-permute-start.1 = (bf16[32,4096]{1,0:T(8,128)(2,1)S(1)}, bf16[32,4096]{1,0:T(8,128)(2,1)S(1)}, u32[]{:S(2)}, u32[]{:S(2)}) collective-permute-start(bf16[32,4096]{1,0:T(8,128)(2,1)S(1)} %tie.9.refs_0_.refs_4_), channel_id=1, source_target_pairs={{0,2},{1,3},{2,0},{3,1},{4,6},{5,7},{6,4},{7,5},{8,10},{9,11},{10,... | collective-permute-start | bytes 786440 | tf_op jit(solution)/shard_map/ppermute | solution.py:383
  18.5 9.4 %collective-permute-start.5 = (bf16[32,4096]{1,0:T(8,128)(2,1)S(1)}, bf16[32,4096]{1,0:T(8,128)(2,1)S(1)}, u32[]{:S(2)}, u32[]{:S(2)}) collective-permute-start(bf16[32,4096]{1,0:T(8,128)(2,1)S(1)} %tie.9.refs_0_.refs_4_), channel_id=1, source_target_pairs={{0,1},{1,0},{2,3},{3,2},{4,5},{5,4},{6,7},{7,6},{8,9},{9,8},{10,11... | collective-permute-start | bytes 786440 | tf_op jit(solution)/shard_map/ppermute | solution.py:383
  21.3 8.8 %collective-permute-start.7 = (bf16[128,1792]{1,0:T(8,128)(2,1)S(1)}, bf16[128,1792]{1,0:T(8,128)(2,1)S(1)}, u32[]{:S(2)}, u32[]{:S(2)}) collective-permute-start(bf16[128,1792]{1,0:T(8,128)(2,1)S(1)} %held_pairs.4.refs_5_), channel_id=1, source_target_pairs={{0,8},{1,17},{2,10},{3,19},{4,12},{5,21},{6,14},{7,23},{8,0},{9,25... | collective-permute-start | bytes 1376264 | tf_op jit(solution)/shard_map/ppermute | solution.py:383
  26.5 1.5 %collective-permute-start.6 = (bf16[32,4096]{1,0:T(8,128)(2,1)S(1)}, bf16[32,4096]{1,0:T(8,128)(2,1)S(1)}, u32[]{:S(2)}, u32[]{:S(2)}) collective-permute-start(bf16[32,4096]{1,0:T(8,128)(2,1)S(1)} %tie.11.refs_1_.refs_5_), channel_id=1, source_target_pairs={{0,1},{1,0},{2,3},{3,2},{4,5},{5,4},{6,7},{7,6},{8,9},{9,8},{10,11... | collective-permute-start | bytes 786440 | tf_op jit(solution)/shard_map/ppermute | solution.py:383
  26.5 12.1 %collective-permute-start.9 = (bf16[128,1792]{1,0:T(8,128)(2,1)S(1)}, bf16[128,1792]{1,0:T(8,128)(2,1)S(1)}, u32[]{:S(2)}, u32[]{:S(2)}) collective-permute-start(bf16[128,1792]{1,0:T(8,128)(2,1)S(1)} %held_pairs.5.refs_1_.refs_13_), channel_id=1, source_target_pairs={{0,8},{1,17},{2,10},{3,19},{4,12},{5,21},{6,14},{7,23},{8,0},{9,25... | collective-permute-start | bytes 1376264 | tf_op jit(solution)/shard_map/ppermute | solution.py:383
  30.1 9.8 %collective-permute-start.8 = (bf16[128,1792]{1,0:T(8,128)(2,1)S(1)}, bf16[128,1792]{1,0:T(8,128)(2,1)S(1)}, u32[]{:S(2)}, u32[]{:S(2)}) collective-permute-start(bf16[128,1792]{1,0:T(8,128)(2,1)S(1)} %tie.12.refs_12_), channel_id=1, source_target_pairs={{0,8},{1,17},{2,10},{3,19},{4,12},{5,21},{6,14},{7,23},{8,0},{9,25... | collective-permute-start | bytes 1376264 | tf_op jit(solution)/shard_map/ppermute | solution.py:383
  40.0 18.4 %collective-permute-start.10 = (bf16[256,1792]{1,0:T(8,128)(2,1)S(1)}, bf16[256,1792]{1,0:T(8,128)(2,1)S(1)}, u32[]{:S(2)}, u32[]{:S(2)}) collective-permute-start(bf16[256,1792]{1,0:T(8,128)(2,1)S(1)} %added.1.refs_5_), channel_id=1, source_target_pairs={{0,16},{1,9},{2,18},{3,11},{4,20},{5,13},{6,22},{7,15},{8,24},{9,1... | collective-permute-start | bytes 2752520 | tf_op jit(solution)/shard_map/ppermute | solution.py:383
  43.7 14.2 %collective-permute-start.11 = (bf16[128,1792]{1,0:T(8,128)(2,1)S(1)}, bf16[128,1792]{1,0:T(8,128)(2,1)S(1)}, u32[]{:S(2)}, u32[]{:S(2)}) collective-permute-start(bf16[128,1792]{1,0:T(8,128)(2,1)S(1)} %held_pairs.7.refs_12_), channel_id=1, source_target_pairs={{0,8},{1,17},{2,10},{3,19},{4,12},{5,21},{6,14},{7,23},{8,0},{9,25... | collective-permute-start | bytes 1376264 | tf_op jit(solution)/shard_map/ppermute | solution.py:383
  58.6 9.0 %collective-permute-start.12 = (bf16[128,896]{1,0:T(8,128)(2,1)S(1)}, bf16[128,896]{1,0:T(8,128)(2,1)S(1)}, u32[]{:S(2)}, u32[]{:S(2)}) collective-permute-start(bf16[128,896]{1,0:T(8,128)(2,1)S(1)} %gated.2.refs_0_), channel_id=1, source_target_pairs={{0,16},{1,9},{2,18},{3,11},{4,20},{5,13},{6,22},{7,15},{8,24},{9,1... | collective-permute-start | bytes 688136 | tf_op jit(solution)/shard_map/ppermute | solution.py:383
  60.2 10.1 %collective-permute-start.15 = (bf16[128,896]{1,0:T(8,128)(2,1)S(1)}, bf16[128,896]{1,0:T(8,128)(2,1)S(1)}, u32[]{:S(2)}, u32[]{:S(2)}) collective-permute-start(bf16[128,896]{1,0:T(8,128)(2,1)S(1)} %gated.2.refs_0_), channel_id=1, source_target_pairs={{0,8},{1,17},{2,10},{3,19},{4,12},{5,21},{6,14},{7,23},{8,0},{9,25... | collective-permute-start | bytes 688136 | tf_op jit(solution)/shard_map/ppermute | solution.py:383
  67.6 6.1 %collective-permute-start.14 = (bf16[128,896]{1,0:T(8,128)(2,1)S(1)}, bf16[128,896]{1,0:T(8,128)(2,1)S(1)}, u32[]{:S(2)}, u32[]{:S(2)}) collective-permute-start(bf16[128,896]{1,0:T(8,128)(2,1)S(1)} %tie.13.refs_1_), channel_id=1, source_target_pairs={{0,8},{1,17},{2,10},{3,19},{4,12},{5,21},{6,14},{7,23},{8,0},{9,25... | collective-permute-start | bytes 688136 | tf_op jit(solution)/shard_map/ppermute | solution.py:383
  68.1 7.7 %collective-permute-start.13 = (bf16[128,896]{1,0:T(8,128)(2,1)S(1)}, bf16[128,896]{1,0:T(8,128)(2,1)S(1)}, u32[]{:S(2)}, u32[]{:S(2)}) collective-permute-start(bf16[128,896]{1,0:T(8,128)(2,1)S(1)} %tie.14.refs_0_), channel_id=1, source_target_pairs={{0,16},{1,9},{2,18},{3,11},{4,20},{5,13},{6,22},{7,15},{8,24},{9,1... | collective-permute-start | bytes 688136 | tf_op jit(solution)/shard_map/ppermute | solution.py:383
  68.6 7.5 %collective-permute-start.16 = (bf16[128,896]{1,0:T(8,128)(2,1)S(1)}, bf16[128,896]{1,0:T(8,128)(2,1)S(1)}, u32[]{:S(2)}, u32[]{:S(2)}) collective-permute-start(bf16[128,896]{1,0:T(8,128)(2,1)S(1)} %tie.14.refs_0_), channel_id=1, source_target_pairs={{0,8},{1,17},{2,10},{3,19},{4,12},{5,21},{6,14},{7,23},{8,0},{9,25... | collective-permute-start | bytes 688136 | tf_op jit(solution)/shard_map/ppermute | solution.py:383
  76.1 2.7 %collective-permute-start.18 = (f32[64,4096]{1,0:T(8,128)S(1)}, f32[64,4096]{1,0:T(8,128)S(1)}, u32[]{:S(2)}, u32[]{:S(2)}) collective-permute-start(f32[64,4096]{1,0:T(8,128)S(1)} %tie.15.refs_2_), channel_id=1, source_target_pairs={{0,1},{1,0},{2,3},{3,2},{4,5},{5,4},{6,7},{7,6},{8,9},{9,8},{10,11... | collective-permute-start | bytes 3145736 | tf_op jit(solution)/shard_map/ppermute | solution.py:383
  77.4 6.1 %collective-permute-start.17 = (bf16[128,896]{1,0:T(8,128)(2,1)S(1)}, bf16[128,896]{1,0:T(8,128)(2,1)S(1)}, u32[]{:S(2)}, u32[]{:S(2)}) collective-permute-start(bf16[128,896]{1,0:T(8,128)(2,1)S(1)} %tie.16.refs_0_), channel_id=1, source_target_pairs={{0,8},{1,17},{2,10},{3,19},{4,12},{5,21},{6,14},{7,23},{8,0},{9,25... | collective-permute-start | bytes 688136 | tf_op jit(solution)/shard_map/ppermute | solution.py:383
  78.9 8.6 %collective-permute-start.19 = (bf16[32,4096]{1,0:T(8,128)(2,1)S(1)}, bf16[32,4096]{1,0:T(8,128)(2,1)S(1)}, u32[]{:S(2)}, u32[]{:S(2)}) collective-permute-start(bf16[32,4096]{1,0:T(8,128)(2,1)S(1)} %slice.33.refs_5_), channel_id=1, source_target_pairs={{0,2},{1,3},{2,0},{3,1},{4,6},{5,7},{6,4},{7,5},{8,10},{9,11},{10,... | collective-permute-start | bytes 786440 | tf_op jit(solution)/shard_map/ppermute | solution.py:383
  87.6 2.7 %collective-permute-start.20 = (f32[64,4096]{1,0:T(8,128)S(1)}, f32[64,4096]{1,0:T(8,128)S(1)}, u32[]{:S(2)}, u32[]{:S(2)}) collective-permute-start(f32[64,4096]{1,0:T(8,128)S(1)} %tie.17), channel_id=1, source_target_pairs={{0,1},{1,0},{2,3},{3,2},{4,5},{5,4},{6,7},{7,6},{8,9},{9,8},{10,11... | collective-permute-start | bytes 3145736 | tf_op jit(solution)/shard_map/ppermute | solution.py:383
  87.7 15.3 %collective-permute-start.22 = (bf16[32,4096]{1,0:T(8,128)(2,1)S(1)}, bf16[32,4096]{1,0:T(8,128)(2,1)S(1)}, u32[]{:S(2)}, u32[]{:S(2)}) collective-permute-start(bf16[32,4096]{1,0:T(8,128)(2,1)S(1)} %fusion.2.refs_1_), channel_id=1, source_target_pairs={{0,4},{1,5},{2,6},{3,7},{4,0},{5,1},{6,2},{7,3},{8,12},{9,13},{10,... | collective-permute-start | bytes 786440 | tf_op jit(solution)/shard_map/ppermute | solution.py:383
  90.5 13.3 %collective-permute-start.21 = (bf16[32,4096]{1,0:T(8,128)(2,1)S(1)}, bf16[32,4096]{1,0:T(8,128)(2,1)S(1)}, u32[]{:S(2)}, u32[]{:S(2)}) collective-permute-start(bf16[32,4096]{1,0:T(8,128)(2,1)S(1)} %slice.32), channel_id=1, source_target_pairs={{0,2},{1,3},{2,0},{3,1},{4,6},{5,7},{6,4},{7,5},{8,10},{9,11},{10,... | collective-permute-start | bytes 786440 | tf_op jit(solution)/shard_map/ppermute | solution.py:383

commit v4 on v3

--- a/solution.py
+++ b/solution.py
@@ -441,7 +441,6 @@
     down_first, down_last = load_down(("first", "last"), *source, deps=(close,))
     second = tie(second, down_last)
     last = swap.first(second)
-    close = tie(close, second)
     close_second, close_first = swap.second(close), swap.first(close)
     total = down((distant, second, first), (down_own, down_second, down_first))
     mine, other = down((last,), (down_last,), total, blocks=2)

time: 105 us -> 107 us (1.019)
  waiting for transfers between devices: 23.5 us -> 25.1 us
    ppermute x23, waiting for transfers between devices: 23.5 us -> 25.1 us  [swap(): return lax.ppermute(value, ('row', 'col'), pairs)]
  transfers between devices with their start and end apart: 23 -> 23, of which waited for: 14 -> 12; matrix products, arithmetic and copies ran while one was open for 0% -> 0% of each run, Pallas kernels for 52% -> 51%
where the time goes in v4:
time: 107 us
  Pallas kernels  55 us (51%)
  waiting for transfers between devices  25.1 us (23%)
  starting transfers between devices  25 us (23%)
    ppermute x23, waiting for transfers between devices, swap(): return lax.ppermute(value, ('row', 'col'), pairs)  25.1 us
    ppermute x23, starting transfers between devices, swap(): return lax.ppermute(value, ('row', 'col'), pairs)  25 us
    pallas_call x2, Pallas kernels, stream_pairs(): pl.pallas_call(functools.partial(stream_pairs_kernel, name, len(x), rows)...  13.7 us
    pallas_call x2, Pallas kernels, load_pairs(): pl.pallas_call(functools.partial(load_pairs_kernel, name), in_specs=[HBM_...  12 us
    pallas_call x2, Pallas kernels, load_down(): pl.pallas_call(functools.partial(load_down_kernel, names), in_specs=[HBM_...  11.5 us
    pallas_call x5, Pallas kernels, down(): pl.pallas_call(functools.partial(down_kernel, count, len(total), blocks,...  9.03 us
    pallas_call x4, Pallas kernels, held_pairs(): pl.pallas_call(functools.partial(held_pairs_kernel, len(x)), in_specs=[VM...  8.25 us
  transfers between devices with their start and end apart: 23, of which 12 were waited for; matrix products, arithmetic and copies ran while one was open for 0% of the time, Pallas kernels for 51%

profile of v4, /device:TPU:0, one launch (start us, length us, event | category | flops | bytes accessed | tf_op | source)
XLA Modules:
  0.0 106.5 jit_solution(8354922222209358218)
XLA Ops:
  0.0 3.0 %collective-permute-start.2 = (bf16[32,4096]{1,0:T(8,128)(2,1)}, bf16[32,4096]{1,0:T(8,128)(2,1)S(1)}, u32[]{:S(2)}, u32[]{:S(2)}) collective-permute-start(bf16[32,4096]{1,0:T(8,128)(2,1)} %refs_8_.3), channel_id=1, source_target_pairs={{0,2},{1,3},{2,0},{3,1},{4,6},{5,7},{6,4},{7,5},{8,10},{9,11},{10,... | collective-permute-start | bytes 786440 | tf_op jit(solution)/shard_map/ppermute | solution.py:383
  3.0 2.6 %collective-permute-start = (bf16[32,4096]{1,0:T(8,128)(2,1)}, bf16[32,4096]{1,0:T(8,128)(2,1)S(1)}, u32[]{:S(2)}, u32[]{:S(2)}) collective-permute-start(bf16[32,4096]{1,0:T(8,128)(2,1)} %refs_8_.3), channel_id=1, source_target_pairs={{0,4},{1,5},{2,6},{3,7},{4,0},{5,1},{6,2},{7,3},{8,12},{9,13},{10,... | collective-permute-start | bytes 786440 | tf_op jit(solution)/shard_map/ppermute | solution.py:383
  5.6 6.0 %load_last.1.refs_4_ = bf16[7,4096,256]{2,1,0:T(8,128)(2,1)S(1)} custom-call(s32[32,28]{1,0:T(8,128)} %refs_0_.11, s32[32,28]{1,0:T(8,128)} %refs_1_.7, bf16[4096,3584]{1,0:T(8,128)(2,1)} %refs_2_.7, bf16[4096,3584]{1,0:T(8,128)(2,1)} %refs_3_.7), custom_call_target="tpu_custom_call" | custom-call | bytes 14680064 | tf_op jit(solution)/shard_map/load_last/pallas_call | solution.py:174
  11.6 6.0 %load_first.1.refs_1_.refs_4_ = bf16[7,4096,256]{2,1,0:T(8,128)(2,1)S(1)} custom-call(s32[32,28]{1,0:T(8,128)} %refs_0_.11, s32[32,28]{1,0:T(8,128)} %refs_1_.7, bf16[4096,3584]{1,0:T(8,128)(2,1)} %refs_2_.7, bf16[4096,3584]{1,0:T(8,128)(2,1)} %refs_3_.7, bf16[7,4096,256]{2,1,0:T(8,128)(2,1)S(1)} %load_last.1.refs_4_), custom_call_target="tpu_custom_call" | custom-call | bytes 14680064 | tf_op jit(solution)/shard_map/load_first/pallas_call | solution.py:174
  19.2 2.1 %held_pairs.4.refs_5_ = bf16[128,1792]{1,0:T(8,128)(2,1)S(1)} custom-call(bf16[32,4096]{1,0:T(8,128)(2,1)S(1)} %copy-done, bf16[32,4096]{1,0:T(8,128)(2,1)S(1)} %tie.9.refs_1_.refs_9_, bf16[32,4096]{1,0:T(8,128)(2,1)S(1)} %collective-permute-done.3.refs_2_.refs_10_, bf16[32,4096]{1,0:T(8,128)(2,1)S(1)} %collective-permute-done.4.refs_3_.refs_11_, ...), custom_call_target="tpu_custom_call" | custom-call | flops 1879048192 | bytes 7340032 | tf_op jit(solution)/shard_map/held_pairs/pallas_call | solution.py:199
  21.3 1.6 %collective-permute-start.7 = (bf16[128,1792]{1,0:T(8,128)(2,1)S(1)}, bf16[128,1792]{1,0:T(8,128)(2,1)S(1)}, u32[]{:S(2)}, u32[]{:S(2)}) collective-permute-start(bf16[128,1792]{1,0:T(8,128)(2,1)S(1)} %held_pairs.4.refs_5_), channel_id=1, source_target_pairs={{0,8},{1,17},{2,10},{3,19},{4,12},{5,21},{6,14},{7,23},{8,0},{9,25... | collective-permute-start | bytes 1376264 | tf_op jit(solution)/shard_map/ppermute | solution.py:383
  22.9 2.1 %held_pairs.5.refs_1_.refs_13_ = bf16[128,1792]{1,0:T(8,128)(2,1)S(1)} custom-call(bf16[32,4096]{1,0:T(8,128)(2,1)S(1)} %copy-done, bf16[32,4096]{1,0:T(8,128)(2,1)S(1)} %tie.9.refs_1_.refs_9_, bf16[32,4096]{1,0:T(8,128)(2,1)S(1)} %collective-permute-done.3.refs_2_.refs_10_, bf16[32,4096]{1,0:T(8,128)(2,1)S(1)} %collective-permute-done.4.refs_3_.refs_11_, ...), custom_call_target="tpu_custom_call" | custom-call | flops 1879048192 | bytes 7340032 | tf_op jit(solution)/shard_map/held_pairs/pallas_call | solution.py:199
  28.0 2.1 %held_pairs.6.refs_0_ = bf16[128,1792]{1,0:T(8,128)(2,1)S(1)} custom-call(bf16[32,4096]{1,0:T(8,128)(2,1)S(1)} %tie.8.refs_0_.refs_4_, bf16[32,4096]{1,0:T(8,128)(2,1)S(1)} %tie.10.refs_1_.refs_5_, bf16[32,4096]{1,0:T(8,128)(2,1)S(1)} %collective-permute-done.5.refs_2_.refs_6_, bf16[32,4096]{1,0:T(8,128)(2,1)S(1)} %collective-permute-done.6.refs_3_.refs_7_, ...), custom_call_target="tpu_custom_call" | custom-call | flops 1879048192 | bytes 7340032 | tf_op jit(solution)/shard_map/held_pairs/pallas_call | solution.py:199
  30.1 1.6 %collective-permute-start.8 = (bf16[128,1792]{1,0:T(8,128)(2,1)S(1)}, bf16[128,1792]{1,0:T(8,128)(2,1)S(1)}, u32[]{:S(2)}, u32[]{:S(2)}) collective-permute-start(bf16[128,1792]{1,0:T(8,128)(2,1)S(1)} %tie.11.refs_12_), channel_id=1, source_target_pairs={{0,8},{1,17},{2,10},{3,19},{4,12},{5,21},{6,14},{7,23},{8,0},{9,25... | collective-permute-start | bytes 1376264 | tf_op jit(solution)/shard_map/ppermute | solution.py:383
  31.6 6.9 %stream_second.1.refs_0_ = f32[256,1792]{1,0:T(8,128)S(1)} custom-call(s32[32,28]{1,0:T(8,128)} %refs_0_.11, s32[32,28]{1,0:T(8,128)} %refs_1_.7, bf16[4096,3584]{1,0:T(8,128)(2,1)} %refs_2_.7, bf16[4096,3584]{1,0:T(8,128)(2,1)} %refs_3_.7, bf16[32,4096]{1,0:T(8,128)(2,1)S(1)} %tie.8.refs_0_.refs_4_, bf16[32,4096]{1,0:T(8,128)(2,1)S(1)} %tie.10.refs_1_.refs_5_, ...), custom_call_target="tpu_custom_call" | custom-call | flops 3758096384 | bytes 14680064 | tf_op jit(solution)/shard_map/stream_second/pallas_call | solution.py:234
  40.0 1.6 %collective-permute-start.10 = (bf16[256,1792]{1,0:T(8,128)(2,1)S(1)}, bf16[256,1792]{1,0:T(8,128)(2,1)S(1)}, u32[]{:S(2)}, u32[]{:S(2)}) collective-permute-start(bf16[256,1792]{1,0:T(8,128)(2,1)S(1)} %added.1.refs_5_), channel_id=1, source_target_pairs={{0,16},{1,9},{2,18},{3,11},{4,20},{5,13},{6,22},{7,15},{8,24},{9,1... | collective-permute-start | bytes 2752520 | tf_op jit(solution)/shard_map/ppermute | solution.py:383
  41.6 2.1 %held_pairs.7.refs_12_ = bf16[128,1792]{1,0:T(8,128)(2,1)S(1)} custom-call(bf16[32,4096]{1,0:T(8,128)(2,1)S(1)} %tie.8.refs_0_.refs_4_, bf16[32,4096]{1,0:T(8,128)(2,1)S(1)} %tie.10.refs_1_.refs_5_, bf16[32,4096]{1,0:T(8,128)(2,1)S(1)} %collective-permute-done.5.refs_2_.refs_6_, bf16[32,4096]{1,0:T(8,128)(2,1)S(1)} %collective-permute-done.6.refs_3_.refs_7_, ...), custom_call_target="tpu_custom_call" | custom-call | flops 1879048192 | bytes 7340032 | tf_op jit(solution)/shard_map/held_pairs/pallas_call | solution.py:199
  43.7 1.6 %collective-permute-start.11 = (bf16[128,1792]{1,0:T(8,128)(2,1)S(1)}, bf16[128,1792]{1,0:T(8,128)(2,1)S(1)}, u32[]{:S(2)}, u32[]{:S(2)}) collective-permute-start(bf16[128,1792]{1,0:T(8,128)(2,1)S(1)} %held_pairs.7.refs_12_), channel_id=1, source_target_pairs={{0,8},{1,17},{2,10},{3,19},{4,12},{5,21},{6,14},{7,23},{8,0},{9,25... | collective-permute-start | bytes 1376264 | tf_op jit(solution)/shard_map/ppermute | solution.py:383
  45.2 6.8 %stream_own.1 = (f32[128,1792]{1,0:T(8,128)S(1)}, f32[128,1792]{1,0:T(8,128)S(1)}) custom-call(s32[32,28]{1,0:T(8,128)} %refs_0_.11, s32[32,28]{1,0:T(8,128)} %refs_1_.7, bf16[4096,3584]{1,0:T(8,128)(2,1)} %refs_2_.7, bf16[4096,3584]{1,0:T(8,128)(2,1)} %refs_3_.7, bf16[32,4096]{1,0:T(8,128)(2,1)S(1)} %tie.8.refs_0_.refs_4_, ...), custom_call_target="tpu_custom_call" | custom-call | flops 3758096384 | bytes 14680064 | tf_op jit(solution)/shard_map/stream_own/pallas_call | solution.py:234
  52.1 5.8 %load_down.2 = (bf16[7,128,4096]{2,1,0:T(8,128)(2,1)S(1)}, bf16[7,128,4096]{2,1,0:T(8,128)(2,1)S(1)}) custom-call(s32[28,32]{1,0:T(8,128)} %mask_hbm.3, bf16[3584,4096]{1,0:T(8,128)(2,1)} %down_hbm.3, f32[128,1792]{1,0:T(8,128)S(1)} %get-tuple-element.16.refs_0_.own), custom_call_target="tpu_custom_call" | custom-call | bytes 14680064 | tf_op jit(solution)/shard_map/load_down/pallas_call | solution.py:278
  58.6 1.6 %collective-permute-start.13 = (bf16[128,896]{1,0:T(8,128)(2,1)S(1)}, bf16[128,896]{1,0:T(8,128)(2,1)S(1)}, u32[]{:S(2)}, u32[]{:S(2)}) collective-permute-start(bf16[128,896]{1,0:T(8,128)(2,1)S(1)} %gated.2.refs_0_), channel_id=1, source_target_pairs={{0,16},{1,9},{2,18},{3,11},{4,20},{5,13},{6,22},{7,15},{8,24},{9,1... | collective-permute-start | bytes 688136 | tf_op jit(solution)/shard_map/ppermute | solution.py:383
  61.9 5.7 %load_down.3 = (bf16[7,128,4096]{2,1,0:T(8,128)(2,1)S(1)}, bf16[7,128,4096]{2,1,0:T(8,128)(2,1)S(1)}) custom-call(s32[28,32]{1,0:T(8,128)} %mask_hbm.3, bf16[3584,4096]{1,0:T(8,128)(2,1)} %down_hbm.3, bf16[128,896]{1,0:T(8,128)(2,1)S(1)} %gated.3.refs_0_), custom_call_target="tpu_custom_call" | custom-call | bytes 14680064 | tf_op jit(solution)/shard_map/load_down/pallas_call | solution.py:278
  68.6 1.6 %collective-permute-start.14 = (bf16[128,896]{1,0:T(8,128)(2,1)S(1)}, bf16[128,896]{1,0:T(8,128)(2,1)S(1)}, u32[]{:S(2)}, u32[]{:S(2)}) collective-permute-start(bf16[128,896]{1,0:T(8,128)(2,1)S(1)} %tie.12.refs_1_), channel_id=1, source_target_pairs={{0,8},{1,17},{2,10},{3,19},{4,12},{5,21},{6,14},{7,23},{8,0},{9,25... | collective-permute-start | bytes 688136 | tf_op jit(solution)/shard_map/ppermute | solution.py:383
  70.2 3.2 %down.5.refs_2_ = f32[128,4096]{1,0:T(8,128)S(1)} custom-call(bf16[128,896]{1,0:T(8,128)(2,1)S(1)} %gated.2.refs_0_, bf16[128,896]{1,0:T(8,128)(2,1)S(1)} %tie.12.refs_1_, bf16[128,896]{1,0:T(8,128)(2,1)S(1)} %collective-permute-done.15.refs_2_, bf16[7,128,4096]{2,1,0:T(8,128)(2,1)S(1)} %get-tuple-element.17.refs_0_.refs_3_.refs_1_, ...), custom_call_target="tpu_custom_call" | custom-call | flops 2818572288 | bytes 22020096 | tf_op jit(solution)/shard_map/down/pallas_call | solution.py:318
  73.4 3.3 %collective-permute-done.14.refs_0_ = bf16[128,896]{1,0:T(8,128)(2,1)S(1)} collective-permute-done((bf16[128,896]{1,0:T(8,128)(2,1)S(1)}, bf16[128,896]{1,0:T(8,128)(2,1)S(1)}, u32[]{:S(2)}, u32[]{:S(2)}) %collective-permute-start.14) | collective-permute-done | bytes 229408 | tf_op jit(solution)/shard_map/ppermute | solution.py:383
  82.1 2.1 %down.8.refs_2_ = f32[128,4096]{1,0:T(8,128)S(1)} custom-call(bf16[128,896]{1,0:T(8,128)(2,1)S(1)} %tie.14.refs_0_, bf16[128,896]{1,0:T(8,128)(2,1)S(1)} %collective-permute-done.16.refs_2_.refs_1_, bf16[7,128,4096]{2,1,0:T(8,128)(2,1)S(1)} %get-tuple-element.19.refs_4_.refs_2_, bf16[7,128,4096]{2,1,0:T(8,128)(2,1)S(1)} %get-tuple-element.20.refs_5_.refs_3_, ...), custom_call_target="tpu_custom_call" | custom-call | flops 1879048192 | bytes 14680064 | tf_op jit(solution)/shard_map/down/pallas_call | solution.py:318
  86.7 2.8 %collective-permute-done.19 = bf16[32,4096]{1,0:T(8,128)(2,1)S(1)} collective-permute-done((bf16[32,4096]{1,0:T(8,128)(2,1)S(1)}, bf16[32,4096]{1,0:T(8,128)(2,1)S(1)}, u32[]{:S(2)}, u32[]{:S(2)}) %collective-permute-start.19) | collective-permute-done | bytes 262176 | tf_op jit(solution)/shard_map/ppermute | solution.py:383
  89.6 2.2 %collective-permute-start.22 = (bf16[32,4096]{1,0:T(8,128)(2,1)S(1)}, bf16[32,4096]{1,0:T(8,128)(2,1)S(1)}, u32[]{:S(2)}, u32[]{:S(2)}) collective-permute-start(bf16[32,4096]{1,0:T(8,128)(2,1)S(1)} %fusion.2.refs_1_), channel_id=1, source_target_pairs={{0,4},{1,5},{2,6},{3,7},{4,0},{5,1},{6,2},{7,3},{8,12},{9,13},{10,... | collective-permute-start | bytes 786440 | tf_op jit(solution)/shard_map/ppermute | solution.py:383
  93.7 11.3 %collective-permute-done.22 = bf16[32,4096]{1,0:T(8,128)(2,1)S(1)} collective-permute-done((bf16[32,4096]{1,0:T(8,128)(2,1)S(1)}, bf16[32,4096]{1,0:T(8,128)(2,1)S(1)}, u32[]{:S(2)}, u32[]{:S(2)}) %collective-permute-start.22) | collective-permute-done | bytes 262176 | tf_op jit(solution)/shard_map/ppermute | solution.py:383
  (56 shorter events, 20.9 us)
Async XLA Ops:
  0.0 17.6 %collective-permute-start.2 = (bf16[32,4096]{1,0:T(8,128)(2,1)}, bf16[32,4096]{1,0:T(8,128)(2,1)S(1)}, u32[]{:S(2)}, u32[]{:S(2)}) collective-permute-start(bf16[32,4096]{1,0:T(8,128)(2,1)} %refs_8_.3), channel_id=1, source_target_pairs={{0,2},{1,3},{2,0},{3,1},{4,6},{5,7},{6,4},{7,5},{8,10},{9,11},{10,... | collective-permute-start | bytes 786440 | tf_op jit(solution)/shard_map/ppermute | solution.py:383
  3.0 15.5 %collective-permute-start.3 = (bf16[32,4096]{1,0:T(8,128)(2,1)}, bf16[32,4096]{1,0:T(8,128)(2,1)S(1)}, u32[]{:S(2)}, u32[]{:S(2)}) collective-permute-start(bf16[32,4096]{1,0:T(8,128)(2,1)} %refs_8_.3), channel_id=1, source_target_pairs={{0,1},{1,0},{2,3},{3,2},{4,5},{5,4},{6,7},{7,6},{8,9},{9,8},{10,11... | collective-permute-start | bytes 786440 | tf_op jit(solution)/shard_map/ppermute | solution.py:383
  3.0 15.5 %collective-permute-start = (bf16[32,4096]{1,0:T(8,128)(2,1)}, bf16[32,4096]{1,0:T(8,128)(2,1)S(1)}, u32[]{:S(2)}, u32[]{:S(2)}) collective-permute-start(bf16[32,4096]{1,0:T(8,128)(2,1)} %refs_8_.3), channel_id=1, source_target_pairs={{0,4},{1,5},{2,6},{3,7},{4,0},{5,1},{6,2},{7,3},{8,12},{9,13},{10,... | collective-permute-start | bytes 786440 | tf_op jit(solution)/shard_map/ppermute | solution.py:383
  17.6 1.6 %copy-start = (bf16[32,4096]{1,0:T(8,128)(2,1)S(1)}, bf16[32,4096]{1,0:T(8,128)(2,1)}, u32[]{:S(2)}) copy-start(bf16[32,4096]{1,0:T(8,128)(2,1)} %refs_8_.3) | copy-start | bytes 786436
  17.6 1.6 %collective-permute-start.4 = (bf16[32,4096]{1,0:T(8,128)(2,1)S(1)}, bf16[32,4096]{1,0:T(8,128)(2,1)S(1)}, u32[]{:S(2)}, u32[]{:S(2)}) collective-permute-start(bf16[32,4096]{1,0:T(8,128)(2,1)S(1)} %tie.9.refs_1_.refs_9_), channel_id=1, source_target_pairs={{0,1},{1,0},{2,3},{3,2},{4,5},{5,4},{6,7},{7,6},{8,9},{9,8},{10,11... | collective-permute-start | bytes 786440 | tf_op jit(solution)/shard_map/ppermute | solution.py:383
  18.5 7.9 %collective-permute-start.1 = (bf16[32,4096]{1,0:T(8,128)(2,1)S(1)}, bf16[32,4096]{1,0:T(8,128)(2,1)S(1)}, u32[]{:S(2)}, u32[]{:S(2)}) collective-permute-start(bf16[32,4096]{1,0:T(8,128)(2,1)S(1)} %tie.8.refs_0_.refs_4_), channel_id=1, source_target_pairs={{0,2},{1,3},{2,0},{3,1},{4,6},{5,7},{6,4},{7,5},{8,10},{9,11},{10,... | collective-permute-start | bytes 786440 | tf_op jit(solution)/shard_map/ppermute | solution.py:383
  18.5 9.4 %collective-permute-start.5 = (bf16[32,4096]{1,0:T(8,128)(2,1)S(1)}, bf16[32,4096]{1,0:T(8,128)(2,1)S(1)}, u32[]{:S(2)}, u32[]{:S(2)}) collective-permute-start(bf16[32,4096]{1,0:T(8,128)(2,1)S(1)} %tie.8.refs_0_.refs_4_), channel_id=1, source_target_pairs={{0,1},{1,0},{2,3},{3,2},{4,5},{5,4},{6,7},{7,6},{8,9},{9,8},{10,11... | collective-permute-start | bytes 786440 | tf_op jit(solution)/shard_map/ppermute | solution.py:383
  21.3 8.8 %collective-permute-start.7 = (bf16[128,1792]{1,0:T(8,128)(2,1)S(1)}, bf16[128,1792]{1,0:T(8,128)(2,1)S(1)}, u32[]{:S(2)}, u32[]{:S(2)}) collective-permute-start(bf16[128,1792]{1,0:T(8,128)(2,1)S(1)} %held_pairs.4.refs_5_), channel_id=1, source_target_pairs={{0,8},{1,17},{2,10},{3,19},{4,12},{5,21},{6,14},{7,23},{8,0},{9,25... | collective-permute-start | bytes 1376264 | tf_op jit(solution)/shard_map/ppermute | solution.py:383
  26.5 1.5 %collective-permute-start.6 = (bf16[32,4096]{1,0:T(8,128)(2,1)S(1)}, bf16[32,4096]{1,0:T(8,128)(2,1)S(1)}, u32[]{:S(2)}, u32[]{:S(2)}) collective-permute-start(bf16[32,4096]{1,0:T(8,128)(2,1)S(1)} %tie.10.refs_1_.refs_5_), channel_id=1, source_target_pairs={{0,1},{1,0},{2,3},{3,2},{4,5},{5,4},{6,7},{7,6},{8,9},{9,8},{10,11... | collective-permute-start | bytes 786440 | tf_op jit(solution)/shard_map/ppermute | solution.py:383
  26.5 12.1 %collective-permute-start.9 = (bf16[128,1792]{1,0:T(8,128)(2,1)S(1)}, bf16[128,1792]{1,0:T(8,128)(2,1)S(1)}, u32[]{:S(2)}, u32[]{:S(2)}) collective-permute-start(bf16[128,1792]{1,0:T(8,128)(2,1)S(1)} %held_pairs.5.refs_1_.refs_13_), channel_id=1, source_target_pairs={{0,8},{1,17},{2,10},{3,19},{4,12},{5,21},{6,14},{7,23},{8,0},{9,25... | collective-permute-start | bytes 1376264 | tf_op jit(solution)/shard_map/ppermute | solution.py:383
  30.1 9.8 %collective-permute-start.8 = (bf16[128,1792]{1,0:T(8,128)(2,1)S(1)}, bf16[128,1792]{1,0:T(8,128)(2,1)S(1)}, u32[]{:S(2)}, u32[]{:S(2)}) collective-permute-start(bf16[128,1792]{1,0:T(8,128)(2,1)S(1)} %tie.11.refs_12_), channel_id=1, source_target_pairs={{0,8},{1,17},{2,10},{3,19},{4,12},{5,21},{6,14},{7,23},{8,0},{9,25... | collective-permute-start | bytes 1376264 | tf_op jit(solution)/shard_map/ppermute | solution.py:383
  40.0 18.4 %collective-permute-start.10 = (bf16[256,1792]{1,0:T(8,128)(2,1)S(1)}, bf16[256,1792]{1,0:T(8,128)(2,1)S(1)}, u32[]{:S(2)}, u32[]{:S(2)}) collective-permute-start(bf16[256,1792]{1,0:T(8,128)(2,1)S(1)} %added.1.refs_5_), channel_id=1, source_target_pairs={{0,16},{1,9},{2,18},{3,11},{4,20},{5,13},{6,22},{7,15},{8,24},{9,1... | collective-permute-start | bytes 2752520 | tf_op jit(solution)/shard_map/ppermute | solution.py:383
  43.7 14.2 %collective-permute-start.11 = (bf16[128,1792]{1,0:T(8,128)(2,1)S(1)}, bf16[128,1792]{1,0:T(8,128)(2,1)S(1)}, u32[]{:S(2)}, u32[]{:S(2)}) collective-permute-start(bf16[128,1792]{1,0:T(8,128)(2,1)S(1)} %held_pairs.7.refs_12_), channel_id=1, source_target_pairs={{0,8},{1,17},{2,10},{3,19},{4,12},{5,21},{6,14},{7,23},{8,0},{9,25... | collective-permute-start | bytes 1376264 | tf_op jit(solution)/shard_map/ppermute | solution.py:383
  58.6 10.0 %collective-permute-start.13 = (bf16[128,896]{1,0:T(8,128)(2,1)S(1)}, bf16[128,896]{1,0:T(8,128)(2,1)S(1)}, u32[]{:S(2)}, u32[]{:S(2)}) collective-permute-start(bf16[128,896]{1,0:T(8,128)(2,1)S(1)} %gated.2.refs_0_), channel_id=1, source_target_pairs={{0,16},{1,9},{2,18},{3,11},{4,20},{5,13},{6,22},{7,15},{8,24},{9,1... | collective-permute-start | bytes 688136 | tf_op jit(solution)/shard_map/ppermute | solution.py:383
  60.2 10.1 %collective-permute-start.15 = (bf16[128,896]{1,0:T(8,128)(2,1)S(1)}, bf16[128,896]{1,0:T(8,128)(2,1)S(1)}, u32[]{:S(2)}, u32[]{:S(2)}) collective-permute-start(bf16[128,896]{1,0:T(8,128)(2,1)S(1)} %gated.2.refs_0_), channel_id=1, source_target_pairs={{0,8},{1,17},{2,10},{3,19},{4,12},{5,21},{6,14},{7,23},{8,0},{9,25... | collective-permute-start | bytes 688136 | tf_op jit(solution)/shard_map/ppermute | solution.py:383
  67.5 10.4 %collective-permute-start.12 = (bf16[128,896]{1,0:T(8,128)(2,1)S(1)}, bf16[128,896]{1,0:T(8,128)(2,1)S(1)}, u32[]{:S(2)}, u32[]{:S(2)}) collective-permute-start(bf16[128,896]{1,0:T(8,128)(2,1)S(1)} %gated.3.refs_0_), channel_id=1, source_target_pairs={{0,16},{1,9},{2,18},{3,11},{4,20},{5,13},{6,22},{7,15},{8,24},{9,1... | collective-permute-start | bytes 688136 | tf_op jit(solution)/shard_map/ppermute | solution.py:383
  68.2 9.8 %collective-permute-start.16 = (bf16[128,896]{1,0:T(8,128)(2,1)S(1)}, bf16[128,896]{1,0:T(8,128)(2,1)S(1)}, u32[]{:S(2)}, u32[]{:S(2)}) collective-permute-start(bf16[128,896]{1,0:T(8,128)(2,1)S(1)} %gated.3.refs_0_), channel_id=1, source_target_pairs={{0,8},{1,17},{2,10},{3,19},{4,12},{5,21},{6,14},{7,23},{8,0},{9,25... | collective-permute-start | bytes 688136 | tf_op jit(solution)/shard_map/ppermute | solution.py:383
  68.6 8.0 %collective-permute-start.14 = (bf16[128,896]{1,0:T(8,128)(2,1)S(1)}, bf16[128,896]{1,0:T(8,128)(2,1)S(1)}, u32[]{:S(2)}, u32[]{:S(2)}) collective-permute-start(bf16[128,896]{1,0:T(8,128)(2,1)S(1)} %tie.12.refs_1_), channel_id=1, source_target_pairs={{0,8},{1,17},{2,10},{3,19},{4,12},{5,21},{6,14},{7,23},{8,0},{9,25... | collective-permute-start | bytes 688136 | tf_op jit(solution)/shard_map/ppermute | solution.py:383
  78.0 2.7 %collective-permute-start.18 = (f32[64,4096]{1,0:T(8,128)S(1)}, f32[64,4096]{1,0:T(8,128)S(1)}, u32[]{:S(2)}, u32[]{:S(2)}) collective-permute-start(f32[64,4096]{1,0:T(8,128)S(1)} %tie.13.refs_2_), channel_id=1, source_target_pairs={{0,1},{1,0},{2,3},{3,2},{4,5},{5,4},{6,7},{7,6},{8,9},{9,8},{10,11... | collective-permute-start | bytes 3145736 | tf_op jit(solution)/shard_map/ppermute | solution.py:383
  79.3 6.1 %collective-permute-start.17 = (bf16[128,896]{1,0:T(8,128)(2,1)S(1)}, bf16[128,896]{1,0:T(8,128)(2,1)S(1)}, u32[]{:S(2)}, u32[]{:S(2)}) collective-permute-start(bf16[128,896]{1,0:T(8,128)(2,1)S(1)} %tie.14.refs_0_), channel_id=1, source_target_pairs={{0,8},{1,17},{2,10},{3,19},{4,12},{5,21},{6,14},{7,23},{8,0},{9,25... | collective-permute-start | bytes 688136 | tf_op jit(solution)/shard_map/ppermute | solution.py:383
  80.9 8.6 %collective-permute-start.19 = (bf16[32,4096]{1,0:T(8,128)(2,1)S(1)}, bf16[32,4096]{1,0:T(8,128)(2,1)S(1)}, u32[]{:S(2)}, u32[]{:S(2)}) collective-permute-start(bf16[32,4096]{1,0:T(8,128)(2,1)S(1)} %slice.33.refs_5_), channel_id=1, source_target_pairs={{0,2},{1,3},{2,0},{3,1},{4,6},{5,7},{6,4},{7,5},{8,10},{9,11},{10,... | collective-permute-start | bytes 786440 | tf_op jit(solution)/shard_map/ppermute | solution.py:383
  89.6 2.7 %collective-permute-start.20 = (f32[64,4096]{1,0:T(8,128)S(1)}, f32[64,4096]{1,0:T(8,128)S(1)}, u32[]{:S(2)}, u32[]{:S(2)}) collective-permute-start(f32[64,4096]{1,0:T(8,128)S(1)} %tie.15), channel_id=1, source_target_pairs={{0,1},{1,0},{2,3},{3,2},{4,5},{5,4},{6,7},{7,6},{8,9},{9,8},{10,11... | collective-permute-start | bytes 3145736 | tf_op jit(solution)/shard_map/ppermute | solution.py:383
  89.6 15.3 %collective-permute-start.22 = (bf16[32,4096]{1,0:T(8,128)(2,1)S(1)}, bf16[32,4096]{1,0:T(8,128)(2,1)S(1)}, u32[]{:S(2)}, u32[]{:S(2)}) collective-permute-start(bf16[32,4096]{1,0:T(8,128)(2,1)S(1)} %fusion.2.refs_1_), channel_id=1, source_target_pairs={{0,4},{1,5},{2,6},{3,7},{4,0},{5,1},{6,2},{7,3},{8,12},{9,13},{10,... | collective-permute-start | bytes 786440 | tf_op jit(solution)/shard_map/ppermute | solution.py:383
  92.4 13.3 %collective-permute-start.21 = (bf16[32,4096]{1,0:T(8,128)(2,1)S(1)}, bf16[32,4096]{1,0:T(8,128)(2,1)S(1)}, u32[]{:S(2)}, u32[]{:S(2)}) collective-permute-start(bf16[32,4096]{1,0:T(8,128)(2,1)S(1)} %slice.32), channel_id=1, source_target_pairs={{0,2},{1,3},{2,0},{3,1},{4,6},{5,7},{6,4},{7,5},{8,10},{9,11},{10,... | collective-permute-start | bytes 786440 | tf_op jit(solution)/shard_map/ppermute | solution.py:383
